TPU v7x, 128 devices: a whole 4x4x4 slice. The times are simulated.
128 devices in a mesh: region: 8 (over y, core), dev: 16 (over x, z).
Axes of the slice: x: 4, y: 4, z: 4, core: 2. Of those that a mesh axis runs over, the one named last changes fastest.
Arguments:
- a_vals: bfloat16 [16384, 16, 4096], P(('region', 'dev')), may hold values from -0.75 to 0.75
- a_cols: int32 [16384, 16], P(('region', 'dev')), may hold values from 0 to 2047, as said below
- p_vals: bfloat16 [16384, 2, 4096], P(('region', 'dev')), may hold values from -0.75 to 0.75
- send_slot: int32 [16384, 2, 16, 2], P(('region', 'dev')), may hold values from 0 to 511, as said below
- recv_slot: int32 [128, 512], P(('region', 'dev')), may hold values from 0 to 63
Outputs:
- coarse: float32 [8192, 4096], P(('region', 'dev'))
Inputs may be any that keep to these rules, and one draw needn't show every extreme that they name: `a_cols`: each row's first entry is the row itself; every entry names a row of the same device or of the devices just before and after it along dev in the same region. `send_slot`: most terms go to owners in the row's own region; some slots may stay empty.
All inputs are finite; a program needn't handle non-finite values.
Results may differ from a plain program's by a relative error of at most 0.0029.
Values may be sent and summed in bfloat16 or wider, within the bound.
A program may use at most 256 MiB of HBM per device.

v0:
```python
import jax
import jax.numpy as jnp
from jax import lax
from jax.sharding import PartitionSpec as P

B = 64
CAP = 4
SLOTS = 64


def with_halo(block, sides, width):
    for axis, dim in sides:
        count = lax.axis_size(axis)
        forward = [(i, i + 1) for i in range(count - 1)]
        backward = [(target, source) for source, target in forward]
        low = lax.ppermute(
            lax.slice_in_dim(block, block.shape[dim] - width, None, axis=dim), axis, forward
        )
        high = lax.ppermute(lax.slice_in_dim(block, 0, width, axis=dim), axis, backward)
        block = jnp.concatenate([low, block, high], axis=dim)
    return block


def bucket_sums(a_vals, position, nearby, p_vals, send_slot, first_row, row_total, bucket_count):
    a_blocks = a_vals.shape[1]
    p_blocks = p_vals.shape[1]
    tile_area = B * B
    stride = min(row_total, 16)

    def advance(totals, turn_index):
        start_row = first_row + turn_index * stride
        a_part = lax.dynamic_slice_in_dim(a_vals, start_row, stride, 0).reshape(
            stride, a_blocks, 1, B, B
        )
        a_wide = jnp.broadcast_to(a_part, (stride, a_blocks, p_blocks, B, B))
        pos_part = lax.dynamic_slice_in_dim(position, start_row, stride, 0)
        right_rows = jnp.take(nearby, pos_part, axis=0).reshape(stride, a_blocks, p_blocks, B, B)
        inner_tiles = lax.dot_general(
            a_wide,
            right_rows,
            (((4,), (3,)), ((0, 1, 2), (0, 1, 2))),
            preferred_element_type=jnp.float32,
        ).astype(jnp.bfloat16)
        own_rows = lax.dynamic_slice_in_dim(p_vals, start_row, stride, 0).reshape(
            stride, p_blocks, 1, 1, B, B
        )
        left_wide = jnp.broadcast_to(own_rows, (stride, p_blocks, a_blocks, p_blocks, B, B))
        right_wide = jnp.broadcast_to(
            inner_tiles[:, None], (stride, p_blocks, a_blocks, p_blocks, B, B)
        )
        tile_terms = lax.dot_general(
            left_wide,
            right_wide,
            (((4,), (4,)), ((0, 1, 2, 3), (0, 1, 2, 3))),
            preferred_element_type=jnp.float32,
        )
        slot_part = lax.dynamic_slice_in_dim(send_slot, start_row, stride, 0)
        added = jax.ops.segment_sum(
            tile_terms.reshape(-1, tile_area), slot_part.reshape(-1), num_segments=bucket_count
        )
        return (totals + added, None)

    start_totals = jnp.zeros((bucket_count, tile_area), jnp.float32)
    totals, _ = lax.scan(advance, start_totals, jnp.arange(row_total // stride, dtype=jnp.int32))
    return totals


def deliver(totals, recv_slot):
    tile_area = B * B
    regions = lax.axis_size("region")
    devices = lax.axis_size("dev")
    arrived = lax.all_to_all(
        totals.reshape(regions * devices, CAP, tile_area),
        ("region", "dev"),
        split_axis=0,
        concat_axis=0,
        tiled=True,
    )
    return jax.ops.segment_sum(
        arrived.reshape(-1, tile_area), recv_slot.reshape(-1), num_segments=SLOTS
    )


def shards(a_vals, a_cols, p_vals, send_slot, recv_slot):
    row_count = a_vals.shape[0]
    bucket_count = lax.axis_size("region") * lax.axis_size("dev") * CAP
    nearby = with_halo(p_vals, (("dev", 0),), row_count)
    offset = (lax.axis_index("dev") - 1) * row_count
    position = a_cols - offset
    all_sums = bucket_sums(a_vals, position, nearby, p_vals, send_slot, 0, row_count, bucket_count)
    coarse = deliver(all_sums, recv_slot)
    return coarse


def solution(mesh):
    in_specs = (
        P(("region", "dev"), None, None),
        P(("region", "dev"), None),
        P(("region", "dev"), None, None),
        P(("region", "dev"), None, None, None),
        P(("region", "dev"), None),
    )
    out_specs = P(("region", "dev"), None)
    return jax.shard_map(shards, mesh=mesh, in_specs=in_specs, out_specs=out_specs, check_vma=False)
```

profile of v0, /device:TPU:1, one launch (start us, length us, event | category | flops | bytes accessed | tf_op | source)
XLA Modules:
  0.0 1247.2 jit_solution(7802210894399516015)
XLA Ops:
  6.6 42.3 %collective-permute-done = bf16[128,2,4096]{2,1,0:T(2,128)(2,1)S(1)} collective-permute-done((bf16[128,2,4096]{2,1,0:T(2,128)(2,1)}, bf16[128,2,4096]{2,1,0:T(2,128)(2,1)S(1)}, u32[]{:S(2)}, u32[]{:S(2)}) %collective-permute-start) | collective-permute-done | bytes 2097184 | tf_op jit(solution)/shard_map/ppermute | solution.py:16
  53.0 23.5 %pad_maximum_fusion = bf16[384,2,4096]{2,1,0:T(2,128)(2,1)} fusion(bf16[128,2,4096]{2,1,0:T(2,128)(2,1)} %collective-permute-done.1, bf16[128,2,4096]{2,1,0:T(2,128)(2,1)} %param.9, bf16[128,2,4096]{2,1,0:T(2,128)(2,1)S(1)} %collective-permute-done), kind=kLoop, calls=%fused_computation.19 | loop fusion | flops 6291456 | bytes 12582912 | tf_op jit(solution)/shard_map/concatenate | solution.py:20
  80.7 1021.8 %while.10 = (s32[]{:T(128)}, f32[512,4096]{1,0:T(8,128)}, s32[8]{0:T(128)S(1)}, s32[128,2,16,2]{0,3,2,1:T(2,128)S(1)}, bf16[128,2,4096]{2,1,0:T(2,128)(2,1)}, /*...) while((s32[]{:T(128)}, f32[512,4096]{1,0:T(8,128)}, ...), condition=%wide.region_2.3_spmd, body=%wide.region_0.2_spmd.sunk | while | flops 813697536 | bytes 142383808 | solution.py:64
  96.9 16.9 %gather_fusion = bf16[256,2,4096]{2,1,0:T(2,128)(2,1)} fusion(bf16[384,2,4096]{2,1,0:T(2,128)(2,1)} %get-tuple-element.158, s32[1024]{0:T(1024)S(1)} %pad_clamp_fusion.2), kind=kCustom, calls=%fused_computation.clone.1 | custom fusion | bytes 8389632 | tf_op jit(solution)/shard_map/while/body/eval_jaxpr/jit(_take)/gather | solution.py:37
  113.8 14.2 %gather.11 = bf16[16,16,2,64,64]{4,3,2,1,0:T(8,128)(2,1)} reshape(bf16[256,2,4096]{2,1,0:T(2,128)(2,1)} %gather_fusion) | data formatting | bytes 8388608 | tf_op jit(solution)/shard_map/while/body/eval_jaxpr/jit(_take)/gather | solution.py:37
  144.9 14.7 %fusion.25 = f32[16,2,16,2,64,64]{5,4,3,2,1,0:T(8,128)} fusion(bf16[16,16,2,64,64]{4,3,2,1,0:T(8,128)(2,1)} %fusion.24, bf16[16,2,64,64]{2,3,1,0:T(8,128)(2,1)S(1)} %copy.18), kind=kOutput, calls=%fused_computation.3.clone.1 | convolution fusion | flops 536870912 | bytes 21233664 | tf_op jit(solution)/shard_map/while/body/eval_jaxpr/dot_general | solution.py:51
  159.6 27.9 %reshape.75 = f32[1024,4096]{1,0:T(8,128)} reshape(f32[16,2,16,2,64,64]{5,4,3,2,1,0:T(8,128)} %fusion.25) | data formatting | bytes 33554432 | tf_op jit(solution)/shard_map/while/body/eval_jaxpr/reshape | solution.py:59
  188.2 33.2 %scatter_fusion = f32[512,4096]{1,0:T(8,128)} fusion(f32[512,4096]{1,0:T(8,128)} %get-tuple-element.140, s32[1024]{0:T(1024)S(1)} %reshape.72, f32[1024,4096]{1,0:T(8,128)} %reshape.75), kind=kCustom, calls=%fused_computation.1.clone.1 | custom fusion | flops 4194304 | bytes 50335744 | tf_op jit(solution)/shard_map/while/body/eval_jaxpr/scatter-add | solution.py:58
  222.8 16.9 %gather_fusion = bf16[256,2,4096]{2,1,0:T(2,128)(2,1)} fusion(bf16[384,2,4096]{2,1,0:T(2,128)(2,1)} %get-tuple-element.158, s32[1024]{0:T(1024)S(1)} %pad_clamp_fusion.2), kind=kCustom, calls=%fused_computation.clone.1 | custom fusion | bytes 8389632 | tf_op jit(solution)/shard_map/while/body/eval_jaxpr/jit(_take)/gather | solution.py:37
  239.7 14.2 %gather.11 = bf16[16,16,2,64,64]{4,3,2,1,0:T(8,128)(2,1)} reshape(bf16[256,2,4096]{2,1,0:T(2,128)(2,1)} %gather_fusion) | data formatting | bytes 8388608 | tf_op jit(solution)/shard_map/while/body/eval_jaxpr/jit(_take)/gather | solution.py:37
  270.8 14.7 %fusion.25 = f32[16,2,16,2,64,64]{5,4,3,2,1,0:T(8,128)} fusion(bf16[16,16,2,64,64]{4,3,2,1,0:T(8,128)(2,1)} %fusion.24, bf16[16,2,64,64]{2,3,1,0:T(8,128)(2,1)S(1)} %copy.18), kind=kOutput, calls=%fused_computation.3.clone.1 | convolution fusion | flops 536870912 | bytes 21233664 | tf_op jit(solution)/shard_map/while/body/eval_jaxpr/dot_general | solution.py:51
  285.5 27.9 %reshape.75 = f32[1024,4096]{1,0:T(8,128)} reshape(f32[16,2,16,2,64,64]{5,4,3,2,1,0:T(8,128)} %fusion.25) | data formatting | bytes 33554432 | tf_op jit(solution)/shard_map/while/body/eval_jaxpr/reshape | solution.py:59
  314.0 33.2 %scatter_fusion = f32[512,4096]{1,0:T(8,128)} fusion(f32[512,4096]{1,0:T(8,128)} %get-tuple-element.140, s32[1024]{0:T(1024)S(1)} %reshape.72, f32[1024,4096]{1,0:T(8,128)} %reshape.75), kind=kCustom, calls=%fused_computation.1.clone.1 | custom fusion | flops 4194304 | bytes 50335744 | tf_op jit(solution)/shard_map/while/body/eval_jaxpr/scatter-add | solution.py:58
  348.7 16.9 %gather_fusion = bf16[256,2,4096]{2,1,0:T(2,128)(2,1)} fusion(bf16[384,2,4096]{2,1,0:T(2,128)(2,1)} %get-tuple-element.158, s32[1024]{0:T(1024)S(1)} %pad_clamp_fusion.2), kind=kCustom, calls=%fused_computation.clone.1 | custom fusion | bytes 8389632 | tf_op jit(solution)/shard_map/while/body/eval_jaxpr/jit(_take)/gather | solution.py:37
  365.6 14.2 %gather.11 = bf16[16,16,2,64,64]{4,3,2,1,0:T(8,128)(2,1)} reshape(bf16[256,2,4096]{2,1,0:T(2,128)(2,1)} %gather_fusion) | data formatting | bytes 8388608 | tf_op jit(solution)/shard_map/while/body/eval_jaxpr/jit(_take)/gather | solution.py:37
  396.7 14.7 %fusion.25 = f32[16,2,16,2,64,64]{5,4,3,2,1,0:T(8,128)} fusion(bf16[16,16,2,64,64]{4,3,2,1,0:T(8,128)(2,1)} %fusion.24, bf16[16,2,64,64]{2,3,1,0:T(8,128)(2,1)S(1)} %copy.18), kind=kOutput, calls=%fused_computation.3.clone.1 | convolution fusion | flops 536870912 | bytes 21233664 | tf_op jit(solution)/shard_map/while/body/eval_jaxpr/dot_general | solution.py:51
  411.4 27.9 %reshape.75 = f32[1024,4096]{1,0:T(8,128)} reshape(f32[16,2,16,2,64,64]{5,4,3,2,1,0:T(8,128)} %fusion.25) | data formatting | bytes 33554432 | tf_op jit(solution)/shard_map/while/body/eval_jaxpr/reshape | solution.py:59
  439.9 33.2 %scatter_fusion = f32[512,4096]{1,0:T(8,128)} fusion(f32[512,4096]{1,0:T(8,128)} %get-tuple-element.140, s32[1024]{0:T(1024)S(1)} %reshape.72, f32[1024,4096]{1,0:T(8,128)} %reshape.75), kind=kCustom, calls=%fused_computation.1.clone.1 | custom fusion | flops 4194304 | bytes 50335744 | tf_op jit(solution)/shard_map/while/body/eval_jaxpr/scatter-add | solution.py:58
  474.6 16.9 %gather_fusion = bf16[256,2,4096]{2,1,0:T(2,128)(2,1)} fusion(bf16[384,2,4096]{2,1,0:T(2,128)(2,1)} %get-tuple-element.158, s32[1024]{0:T(1024)S(1)} %pad_clamp_fusion.2), kind=kCustom, calls=%fused_computation.clone.1 | custom fusion | bytes 8389632 | tf_op jit(solution)/shard_map/while/body/eval_jaxpr/jit(_take)/gather | solution.py:37
  491.4 14.2 %gather.11 = bf16[16,16,2,64,64]{4,3,2,1,0:T(8,128)(2,1)} reshape(bf16[256,2,4096]{2,1,0:T(2,128)(2,1)} %gather_fusion) | data formatting | bytes 8388608 | tf_op jit(solution)/shard_map/while/body/eval_jaxpr/jit(_take)/gather | solution.py:37
  512.9 7.9 fusion.24
  522.6 14.7 %fusion.25 = f32[16,2,16,2,64,64]{5,4,3,2,1,0:T(8,128)} fusion(bf16[16,16,2,64,64]{4,3,2,1,0:T(8,128)(2,1)} %fusion.24, bf16[16,2,64,64]{2,3,1,0:T(8,128)(2,1)S(1)} %copy.18), kind=kOutput, calls=%fused_computation.3.clone.1 | convolution fusion | flops 536870912 | bytes 21233664 | tf_op jit(solution)/shard_map/while/body/eval_jaxpr/dot_general | solution.py:51
  537.3 27.9 %reshape.75 = f32[1024,4096]{1,0:T(8,128)} reshape(f32[16,2,16,2,64,64]{5,4,3,2,1,0:T(8,128)} %fusion.25) | data formatting | bytes 33554432 | tf_op jit(solution)/shard_map/while/body/eval_jaxpr/reshape | solution.py:59
  565.8 33.2 %scatter_fusion = f32[512,4096]{1,0:T(8,128)} fusion(f32[512,4096]{1,0:T(8,128)} %get-tuple-element.140, s32[1024]{0:T(1024)S(1)} %reshape.72, f32[1024,4096]{1,0:T(8,128)} %reshape.75), kind=kCustom, calls=%fused_computation.1.clone.1 | custom fusion | flops 4194304 | bytes 50335744 | tf_op jit(solution)/shard_map/while/body/eval_jaxpr/scatter-add | solution.py:58
  600.5 16.9 %gather_fusion = bf16[256,2,4096]{2,1,0:T(2,128)(2,1)} fusion(bf16[384,2,4096]{2,1,0:T(2,128)(2,1)} %get-tuple-element.158, s32[1024]{0:T(1024)S(1)} %pad_clamp_fusion.2), kind=kCustom, calls=%fused_computation.clone.1 | custom fusion | bytes 8389632 | tf_op jit(solution)/shard_map/while/body/eval_jaxpr/jit(_take)/gather | solution.py:37
  617.3 14.2 %gather.11 = bf16[16,16,2,64,64]{4,3,2,1,0:T(8,128)(2,1)} reshape(bf16[256,2,4096]{2,1,0:T(2,128)(2,1)} %gather_fusion) | data formatting | bytes 8388608 | tf_op jit(solution)/shard_map/while/body/eval_jaxpr/jit(_take)/gather | solution.py:37
  648.4 14.7 %fusion.25 = f32[16,2,16,2,64,64]{5,4,3,2,1,0:T(8,128)} fusion(bf16[16,16,2,64,64]{4,3,2,1,0:T(8,128)(2,1)} %fusion.24, bf16[16,2,64,64]{2,3,1,0:T(8,128)(2,1)S(1)} %copy.18), kind=kOutput, calls=%fused_computation.3.clone.1 | convolution fusion | flops 536870912 | bytes 21233664 | tf_op jit(solution)/shard_map/while/body/eval_jaxpr/dot_general | solution.py:51
  663.2 27.9 %reshape.75 = f32[1024,4096]{1,0:T(8,128)} reshape(f32[16,2,16,2,64,64]{5,4,3,2,1,0:T(8,128)} %fusion.25) | data formatting | bytes 33554432 | tf_op jit(solution)/shard_map/while/body/eval_jaxpr/reshape | solution.py:59
  691.7 33.2 %scatter_fusion = f32[512,4096]{1,0:T(8,128)} fusion(f32[512,4096]{1,0:T(8,128)} %get-tuple-element.140, s32[1024]{0:T(1024)S(1)} %reshape.72, f32[1024,4096]{1,0:T(8,128)} %reshape.75), kind=kCustom, calls=%fused_computation.1.clone.1 | custom fusion | flops 4194304 | bytes 50335744 | tf_op jit(solution)/shard_map/while/body/eval_jaxpr/scatter-add | solution.py:58
  726.4 16.9 %gather_fusion = bf16[256,2,4096]{2,1,0:T(2,128)(2,1)} fusion(bf16[384,2,4096]{2,1,0:T(2,128)(2,1)} %get-tuple-element.158, s32[1024]{0:T(1024)S(1)} %pad_clamp_fusion.2), kind=kCustom, calls=%fused_computation.clone.1 | custom fusion | bytes 8389632 | tf_op jit(solution)/shard_map/while/body/eval_jaxpr/jit(_take)/gather | solution.py:37
  743.2 14.2 %gather.11 = bf16[16,16,2,64,64]{4,3,2,1,0:T(8,128)(2,1)} reshape(bf16[256,2,4096]{2,1,0:T(2,128)(2,1)} %gather_fusion) | data formatting | bytes 8388608 | tf_op jit(solution)/shard_map/while/body/eval_jaxpr/jit(_take)/gather | solution.py:37
  774.3 14.7 %fusion.25 = f32[16,2,16,2,64,64]{5,4,3,2,1,0:T(8,128)} fusion(bf16[16,16,2,64,64]{4,3,2,1,0:T(8,128)(2,1)} %fusion.24, bf16[16,2,64,64]{2,3,1,0:T(8,128)(2,1)S(1)} %copy.18), kind=kOutput, calls=%fused_computation.3.clone.1 | convolution fusion | flops 536870912 | bytes 21233664 | tf_op jit(solution)/shard_map/while/body/eval_jaxpr/dot_general | solution.py:51
  789.0 27.9 %reshape.75 = f32[1024,4096]{1,0:T(8,128)} reshape(f32[16,2,16,2,64,64]{5,4,3,2,1,0:T(8,128)} %fusion.25) | data formatting | bytes 33554432 | tf_op jit(solution)/shard_map/while/body/eval_jaxpr/reshape | solution.py:59
  817.6 33.2 %scatter_fusion = f32[512,4096]{1,0:T(8,128)} fusion(f32[512,4096]{1,0:T(8,128)} %get-tuple-element.140, s32[1024]{0:T(1024)S(1)} %reshape.72, f32[1024,4096]{1,0:T(8,128)} %reshape.75), kind=kCustom, calls=%fused_computation.1.clone.1 | custom fusion | flops 4194304 | bytes 50335744 | tf_op jit(solution)/shard_map/while/body/eval_jaxpr/scatter-add | solution.py:58
  852.2 16.9 %gather_fusion = bf16[256,2,4096]{2,1,0:T(2,128)(2,1)} fusion(bf16[384,2,4096]{2,1,0:T(2,128)(2,1)} %get-tuple-element.158, s32[1024]{0:T(1024)S(1)} %pad_clamp_fusion.2), kind=kCustom, calls=%fused_computation.clone.1 | custom fusion | bytes 8389632 | tf_op jit(solution)/shard_map/while/body/eval_jaxpr/jit(_take)/gather | solution.py:37
  869.1 14.2 %gather.11 = bf16[16,16,2,64,64]{4,3,2,1,0:T(8,128)(2,1)} reshape(bf16[256,2,4096]{2,1,0:T(2,128)(2,1)} %gather_fusion) | data formatting | bytes 8388608 | tf_op jit(solution)/shard_map/while/body/eval_jaxpr/jit(_take)/gather | solution.py:37
  900.2 14.7 %fusion.25 = f32[16,2,16,2,64,64]{5,4,3,2,1,0:T(8,128)} fusion(bf16[16,16,2,64,64]{4,3,2,1,0:T(8,128)(2,1)} %fusion.24, bf16[16,2,64,64]{2,3,1,0:T(8,128)(2,1)S(1)} %copy.18), kind=kOutput, calls=%fused_computation.3.clone.1 | convolution fusion | flops 536870912 | bytes 21233664 | tf_op jit(solution)/shard_map/while/body/eval_jaxpr/dot_general | solution.py:51
  914.9 27.9 %reshape.75 = f32[1024,4096]{1,0:T(8,128)} reshape(f32[16,2,16,2,64,64]{5,4,3,2,1,0:T(8,128)} %fusion.25) | data formatting | bytes 33554432 | tf_op jit(solution)/shard_map/while/body/eval_jaxpr/reshape | solution.py:59
  943.5 33.2 %scatter_fusion = f32[512,4096]{1,0:T(8,128)} fusion(f32[512,4096]{1,0:T(8,128)} %get-tuple-element.140, s32[1024]{0:T(1024)S(1)} %reshape.72, f32[1024,4096]{1,0:T(8,128)} %reshape.75), kind=kCustom, calls=%fused_computation.1.clone.1 | custom fusion | flops 4194304 | bytes 50335744 | tf_op jit(solution)/shard_map/while/body/eval_jaxpr/scatter-add | solution.py:58
  978.1 16.9 %gather_fusion = bf16[256,2,4096]{2,1,0:T(2,128)(2,1)} fusion(bf16[384,2,4096]{2,1,0:T(2,128)(2,1)} %get-tuple-element.158, s32[1024]{0:T(1024)S(1)} %pad_clamp_fusion.2), kind=kCustom, calls=%fused_computation.clone.1 | custom fusion | bytes 8389632 | tf_op jit(solution)/shard_map/while/body/eval_jaxpr/jit(_take)/gather | solution.py:37
  995.0 14.2 %gather.11 = bf16[16,16,2,64,64]{4,3,2,1,0:T(8,128)(2,1)} reshape(bf16[256,2,4096]{2,1,0:T(2,128)(2,1)} %gather_fusion) | data formatting | bytes 8388608 | tf_op jit(solution)/shard_map/while/body/eval_jaxpr/jit(_take)/gather | solution.py:37
  1026.1 14.7 %fusion.25 = f32[16,2,16,2,64,64]{5,4,3,2,1,0:T(8,128)} fusion(bf16[16,16,2,64,64]{4,3,2,1,0:T(8,128)(2,1)} %fusion.24, bf16[16,2,64,64]{2,3,1,0:T(8,128)(2,1)S(1)} %copy.18), kind=kOutput, calls=%fused_computation.3.clone.1 | convolution fusion | flops 536870912 | bytes 21233664 | tf_op jit(solution)/shard_map/while/body/eval_jaxpr/dot_general | solution.py:51
  1040.8 27.9 %reshape.75 = f32[1024,4096]{1,0:T(8,128)} reshape(f32[16,2,16,2,64,64]{5,4,3,2,1,0:T(8,128)} %fusion.25) | data formatting | bytes 33554432 | tf_op jit(solution)/shard_map/while/body/eval_jaxpr/reshape | solution.py:59
  1069.3 33.2 %scatter_fusion = f32[512,4096]{1,0:T(8,128)} fusion(f32[512,4096]{1,0:T(8,128)} %get-tuple-element.140, s32[1024]{0:T(1024)S(1)} %reshape.72, f32[1024,4096]{1,0:T(8,128)} %reshape.75), kind=kCustom, calls=%fused_computation.1.clone.1 | custom fusion | flops 4194304 | bytes 50335744 | tf_op jit(solution)/shard_map/while/body/eval_jaxpr/scatter-add | solution.py:58
  1102.5 9.8 reshape.26
  1112.3 109.6 %all_to_all.5 = f32[128,4,4096]{2,1,0:T(4,128)} all-to-all(f32[128,4,4096]{2,1,0:T(4,128)} %reshape.26), channel_id=1, replica_groups=mesh['region'=8,'dev'=16] {'region','dev'}, dimensions={0} | all-to-all | bytes 16777216 | tf_op jit(solution)/shard_map/all_to_all | solution.py:72
  1221.9 10.0 reshape.48
  1231.9 14.9 %scatter_custom_fusion.1 = f32[64,4096]{1,0:T(8,128)} fusion(s32[512]{0:T(512)} %bitcast.8, f32[512,4096]{1,0:T(8,128)} %reshape.48, f32[]{:T(128)} %constant.11.clone.1), kind=kCustom, calls=%fused_computation.20 | custom fusion | flops 2097152 | bytes 1049088 | tf_op jit(solution)/shard_map/scatter-add | solution.py:79
  (112 shorter events, 153.1 us)
Async XLA Ops:
  0.0 49.0 %collective-permute-start = (bf16[128,2,4096]{2,1,0:T(2,128)(2,1)}, bf16[128,2,4096]{2,1,0:T(2,128)(2,1)S(1)}, u32[]{:S(2)}, u32[]{:S(2)}) collective-permute-start(bf16[128,2,4096]{2,1,0:T(2,128)(2,1)} %param.9), channel_id=1, source_target_pairs={{0,1},{1,2},{2,3},{3,4},{4,5},{5,6},{6,7},{7,8},{8,9},{9,10},{10,1... | collective-permute-start | bytes 6291464 | tf_op jit(solution)/shard_map/ppermute | solution.py:16
  4.5 48.5 %collective-permute-start.1 = (bf16[128,2,4096]{2,1,0:T(2,128)(2,1)}, bf16[128,2,4096]{2,1,0:T(2,128)(2,1)}, u32[]{:S(2)}, u32[]{:S(2)}) collective-permute-start(bf16[128,2,4096]{2,1,0:T(2,128)(2,1)} %param.9), channel_id=1, source_target_pairs={{1,0},{2,1},{3,2},{4,3},{5,4},{6,5},{7,6},{8,7},{9,8},{10,9},{11,1... | collective-permute-start | bytes 6291464 | tf_op jit(solution)/shard_map/ppermute | solution.py:19
  6.6 74.1 %copy-start = (s32[128,2,16,2]{0,3,2,1:T(2,128)S(1)}, s32[128,2,16,2]{0,3,2,1:T(2,128)}, u32[]{:S(2)}) copy-start(s32[128,2,16,2]{0,3,2,1:T(2,128)} %param.10) | copy-start | bytes 98308
where the time goes:
time: 1260 us; the launch traced here: 1250 us
  local copies, waits for them, and re-layouts  579 us (46%)
  other arithmetic  304 us (24%)
  matrix products  181 us (14%)
  blocking collectives  110 us (9%)
  waiting for transfers between devices  46.4 us (4%)
  loops' own time  20.8 us (2%)
    scatter-add x8, other arithmetic, advance(): jax.ops.segment_sum(tile_terms.reshape(-1, tile_area), slot_part.reshape(...  266 us
    gather x16, local copies, waits for them, and re-layouts, advance(): jnp.take(nearby, pos_part, axis=0).reshape(stride, a_blocks, p_blocks, B, B)  248 us
    reshape x8, local copies, waits for them, and re-layouts, advance(): tile_terms.reshape(-1, tile_area)  223 us
    dot_general x8, matrix products, advance(): lax.dot_general(left_wide, right_wide, (((4,), (4,)), ((0, 1, 2, 3), (0,...  118 us
    all_to_all x1, blocking collectives, deliver(): lax.all_to_all(totals.reshape(regions * devices, CAP, tile_area), ('regio...  110 us
    dot_general x8, matrix products, advance(): lax.dot_general(a_wide, right_rows, (((4,), (3,)), ((0, 1, 2), (0, 1, 2))...  63.2 us
    broadcast_in_dim x8, local copies, waits for them, and re-layouts, advance(): a_wide = jnp.broadcast_to(a_part, (stride, a_blocks, p_blocks, B, B))  44.1 us
    ppermute x1, waiting for transfers between devices, with_halo(): lax.ppermute(lax.slice_in_dim(block, block.shape[dim] - width, None, axis...  42.3 us
  transfers between devices with their start and end apart: 2, of which 2 were waited for; matrix products, arithmetic and copies ran while one was open for 0% of the time, Pallas kernels for 0%

commit v1 on v0

v1 whole, which is shorter than its diff:
```python
import functools

import jax
import jax.numpy as jnp
from jax import lax
from jax.experimental import pallas as pl
from jax.experimental.pallas import tpu as pltpu
from jax.sharding import PartitionSpec as P

B = 64
CAP = 4
SLOTS = 64
HALF = B // 2
WIDE = 2 * B
ROWS_STEP = 8
BATCH = 4


def left_lanes(shape):
    return lax.broadcasted_iota(jnp.int32, shape, len(shape) - 1) < B


def spread(tile):
    other = jnp.concatenate([tile[:, B:], tile[:, :B]], axis=1)
    left = left_lanes(tile.shape)
    zero = jnp.zeros_like(tile)
    return jnp.concatenate(
        [
            jnp.where(left, tile, zero),
            jnp.where(left, other, zero),
            jnp.where(left, zero, other),
            jnp.where(left, zero, tile),
        ],
        axis=0,
    )


def terms_kernel(a_blocks, cols, slots, a_ref, p_ref, low, own, high, out, right, inner, acc0, acc1, acc2, acc3, sems):
    step = pl.program_id(0)
    rows = own.shape[0]
    accs = ((acc0, acc1), (acc2, acc3))
    copies = [
        pltpu.make_async_copy(source, right.at[pl.ds(n * rows, rows)], sems.at[n])
        for n, source in enumerate((low, own, high))
    ]

    @pl.when(step == 0)
    def _():
        for copy in copies:
            copy.start()

        def clear(n, _):
            for pair in accs:
                for acc in pair:
                    acc[n] = jnp.zeros((HALF, WIDE), jnp.float32)
            return 0

        lax.fori_loop(0, out.shape[0], clear, 0, unroll=4)
        for copy in copies:
            copy.wait()

    def inner_tiles(row):
        first = (step * ROWS_STEP + row) * a_blocks
        for k in range(a_blocks):
            tile = spread(a_ref[row * a_blocks + k])
            lhs = right[pl.ds(2 * cols[first + k], 2)].reshape(2 * HALF, WIDE)
            inner[row, pl.ds(k * B, B)] = jnp.dot(
                lhs, tile, preferred_element_type=jnp.float32
            ).astype(jnp.bfloat16)

    def add_terms(row):
        first = (step * ROWS_STEP + row) * a_blocks
        weights = jnp.concatenate([spread(p_ref[2 * row]), spread(p_ref[2 * row + 1])], axis=1)
        for start in range(0, a_blocks, BATCH):
            terms = jnp.dot(
                inner[row, pl.ds(start * B, BATCH * B)], weights, preferred_element_type=jnp.float32
            )
            for k in range(BATCH):
                at = (first + start + k) * 4
                where = [[slots[at + 2 * q + p] for p in range(2)] for q in range(2)]
                old = [[accs[q][p][where[q][p]] for p in range(2)] for q in range(2)]
                for q in range(2):
                    for p in range(2):
                        top = k * B + p * HALF
                        part = terms[top : top + HALF, q * WIDE : (q + 1) * WIDE]
                        accs[q][p][where[q][p]] = old[q][p] + part

    for row in range(ROWS_STEP):
        inner_tiles(row)
    for row in range(ROWS_STEP):
        add_terms(row)

    @pl.when(step == pl.num_programs(0) - 1)
    def _():
        def finish(n, _):
            out[n] = ((acc0[n] + acc1[n]) + (acc2[n] + acc3[n])).astype(jnp.bfloat16)
            return 0

        lax.fori_loop(0, out.shape[0], finish, 0, unroll=4)


def bucket_sums(a_tiles, cols, slots, p_tiles, low, own, high, buckets):
    row_total = p_tiles.shape[0] // 2
    a_blocks = a_tiles.shape[0] // row_total
    return pl.pallas_call(
        functools.partial(terms_kernel, a_blocks),
        grid_spec=pltpu.PrefetchScalarGridSpec(
            num_scalar_prefetch=2,
            grid=(row_total // ROWS_STEP,),
            in_specs=[
                pl.BlockSpec((ROWS_STEP * a_blocks, HALF, WIDE), lambda i, *_: (i, 0, 0)),
                pl.BlockSpec((ROWS_STEP * 2, HALF, WIDE), lambda i, *_: (i, 0, 0)),
                pl.BlockSpec(memory_space=pl.ANY),
                pl.BlockSpec(memory_space=pl.ANY),
                pl.BlockSpec(memory_space=pl.ANY),
            ],
            out_specs=pl.BlockSpec((buckets, HALF, WIDE), lambda i, *_: (0, 0, 0)),
            scratch_shapes=[pltpu.VMEM((3 * 2 * row_total, HALF, WIDE), jnp.bfloat16)]
            + [pltpu.VMEM((ROWS_STEP, a_blocks * B, WIDE), jnp.bfloat16)]
            + [pltpu.VMEM((buckets, HALF, WIDE), jnp.float32)] * 4
            + [pltpu.SemaphoreType.DMA((3,))],
        ),
        out_shape=jax.ShapeDtypeStruct((buckets, HALF, WIDE), jnp.bfloat16),
        compiler_params=pltpu.CompilerParams(
            dimension_semantics=("arbitrary",), vmem_limit_bytes=58 * 2**20
        ),
        cost_estimate=pl.CostEstimate(
            flops=2**33, bytes_accessed=24 * 2**20, transcendentals=0
        ),
        name="terms",
    )(cols, slots, a_tiles, p_tiles, low, own, high)


def gather_kernel(places, arrived, out):
    out[...] = jnp.zeros_like(out)

    def add(n, _):
        place = places[n]
        out[place] += arrived[n].astype(jnp.float32)
        return 0

    lax.fori_loop(0, arrived.shape[0], add, 0, unroll=4)


def owner_sums(places, arrived):
    return pl.pallas_call(
        gather_kernel,
        in_specs=[
            pl.BlockSpec(memory_space=pltpu.SMEM),
            pl.BlockSpec(memory_space=pltpu.VMEM),
        ],
        out_specs=pl.BlockSpec(memory_space=pltpu.VMEM),
        out_shape=jax.ShapeDtypeStruct((SLOTS, HALF, WIDE), jnp.float32),
        compiler_params=pltpu.CompilerParams(vmem_limit_bytes=32 * 2**20),
        name="owner_sums",
    )(places, arrived)


def shards(a_vals, a_cols, p_vals, send_slot, recv_slot):
    rows, a_blocks, tile_area = a_vals.shape
    owners = lax.axis_size("region") * lax.axis_size("dev")
    buckets = owners * CAP
    count = lax.axis_size("dev")

    turned = jnp.swapaxes(p_vals.reshape(rows * 2, B, B), 1, 2).reshape(rows * 2, HALF, WIDE)
    forward = [(i, i + 1) for i in range(count - 1)]
    low = lax.ppermute(turned, "dev", forward)
    high = lax.ppermute(turned, "dev", [(t, s) for s, t in forward])

    cols = (a_cols - (lax.axis_index("dev") - 1) * rows).reshape(-1)
    slots = jnp.transpose(send_slot, (0, 2, 1, 3)).reshape(-1)
    a_tiles = jnp.transpose(
        a_vals.reshape(rows * a_blocks, B, 2, HALF), (0, 3, 2, 1)
    ).reshape(rows * a_blocks, HALF, WIDE)
    p_tiles = jnp.swapaxes(p_vals.reshape(rows * 2, 2, HALF, B), 1, 2).reshape(rows * 2, HALF, WIDE)
    totals = bucket_sums(a_tiles, cols, slots, p_tiles, low, turned, high, buckets)

    arrived = lax.all_to_all(
        totals, ("region", "dev"), split_axis=0, concat_axis=0, tiled=True
    )
    sums = owner_sums(recv_slot.reshape(-1), arrived)
    return jnp.swapaxes(sums.reshape(SLOTS, B, B), 1, 2).reshape(SLOTS, tile_area)


def solution(mesh):
    in_specs = (
        P(("region", "dev"), None, None),
        P(("region", "dev"), None),
        P(("region", "dev"), None, None),
        P(("region", "dev"), None, None, None),
        P(("region", "dev"), None),
    )
    out_specs = P(("region", "dev"), None)
    return jax.shard_map(shards, mesh=mesh, in_specs=in_specs, out_specs=out_specs, check_vma=False)
```

time: 1260 us -> 366 us (0.29)
  local copies, waits for them, and re-layouts: 579 us -> 238 us
  other arithmetic: 304 us -> 0.01 us
  matrix products: 181 us -> 0 us
  Pallas kernels: 0 us -> 51.4 us
  waiting for transfers between devices: 46.4 us -> 0.01 us
  blocking collectives: 110 us -> 63.9 us
  loops' own time: 20.8 us -> 0 us
    scatter-add x9 -> x0, other arithmetic: 280 us -> none  [the longest x8 266 us: advance(): jax.ops.segment_sum(tile_terms.reshape(-1, tile_area), slot_part.reshape(...]
    gather x16 -> x0, local copies, waits for them, and re-layouts: 248 us -> none  [advance(): jnp.take(nearby, pos_part, axis=0).reshape(stride, a_blocks, p_blocks, B, B)]
    dot_general x16 -> x0, matrix products: 181 us -> none  [the longest x8 118 us: advance(): lax.dot_general(left_wide, right_wide, (((4,), (4,)), ((0, 1, 2, 3), (0,...]
    reshape x18 -> x10, local copies, waits for them, and re-layouts: 244 us -> 115 us  [the longest x1 64 us: shards(): a_vals.reshape(rows * a_blocks, B, 2, HALF)]
    transpose x0 -> x5, local copies, waits for them, and re-layouts: none -> 123 us  [the longest x1 107 us: shards(): jnp.transpose(a_vals.reshape(rows * a_blocks, B, 2, HALF), (0, 3, 2, 1))]
    pallas_call x0 -> x2, Pallas kernels: none -> 51.4 us  [the longest x1 48.7 us: bucket_sums(): pl.pallas_call(functools.partial(terms_kernel, a_blocks), grid_spec=pltpu...]
    broadcast_in_dim x32 -> x0, local copies, waits for them, and re-layouts: 49.7 us -> none  [the longest x8 44.1 us: advance(): a_wide = jnp.broadcast_to(a_part, (stride, a_blocks, p_blocks, B, B))]
    ppermute x2, waiting for transfers between devices: 46.4 us -> 0.01 us  [the longest x1 0.01 us: shards(): low = lax.ppermute(turned, 'dev', forward)]
  transfers between devices with their start and end apart: 2 -> 2, of which waited for: 2 -> 0; matrix products, arithmetic and copies ran while one was open for 0% -> 59% of each run, Pallas kernels for 0% -> 0%
where the time goes in v1:
time: 366 us; the launch traced here: 360 us
  local copies, waits for them, and re-layouts  238 us (65%)
  blocking collectives  63.9 us (17%)
  Pallas kernels  51.4 us (14%)
  starting transfers between devices  6.97 us (2%)
    transpose x1, local copies, waits for them, and re-layouts, shards(): jnp.transpose(a_vals.reshape(rows * a_blocks, B, 2, HALF), (0, 3, 2, 1))  107 us
    reshape x1, local copies, waits for them, and re-layouts, shards(): a_vals.reshape(rows * a_blocks, B, 2, HALF)  64 us
    all_to_all x1, blocking collectives, shards(): lax.all_to_all(totals, ('region', 'dev'), split_axis=0, concat_axis=0, ti...  63.9 us
    pallas_call x1, Pallas kernels, bucket_sums(): pl.pallas_call(functools.partial(terms_kernel, a_blocks), grid_spec=pltpu...  48.7 us
    reshape x1, local copies, waits for them, and re-layouts, shards(): a_tiles = jnp.transpose(a_vals.reshape(rows * a_blocks, B, 2, HALF), (0,...  23.6 us
    transpose x1, local copies, waits for them, and re-layouts, shards(): jnp.swapaxes(p_vals.reshape(rows * 2, B, B), 1, 2)  7.79 us
    reshape x1, local copies, waits for them, and re-layouts, shards(): p_vals.reshape(rows * 2, B, B)  7.79 us
  transfers between devices with their start and end apart: 2, of which 0 were waited for; matrix products, arithmetic and copies ran while one was open for 59% of the time, Pallas kernels for 0%

profile of v1, /device:TPU:1, one launch (start us, length us, event | category | flops | bytes accessed | tf_op | source)
XLA Modules:
  0.0 360.1 jit_solution(17290267666426337645)
XLA Ops:
  0.0 7.8 %reshape.40 = bf16[256,64,64]{2,1,0:T(8,128)(2,1)} reshape(bf16[128,2,4096]{2,1,0:T(2,128)(2,1)} %param.7) | data formatting | bytes 4194304 | tf_op jit(solution)/shard_map/reshape | solution.py:165
  7.8 7.8 %copy.14 = bf16[256,64,64]{0,2,1:T(8,128)(2,1)} copy(bf16[256,64,64]{1,2,0:T(8,128)(2,1)} %bitcast.12) | data formatting | bytes 4194304 | tf_op jit(solution)/shard_map/transpose | solution.py:165
  15.6 0.0 copy-start.1
  15.6 4.7 %copy.15.own = bf16[256,32,128]{2,1,0:T(8,128)(2,1)} copy(bf16[256,32,128]{0,2,1:T(8,128)(2,1)} %bitcast.13) | data formatting | bytes 4194304 | tf_op jit(solution)/shard_map/reshape | solution.py:165
  20.3 5.7 %collective-permute-start = (bf16[256,32,128]{2,1,0:T(8,128)(2,1)}, bf16[256,32,128]{2,1,0:T(8,128)(2,1)}, u32[]{:S(2)}, u32[]{:S(2)}) collective-permute-start(bf16[256,32,128]{2,1,0:T(8,128)(2,1)} %copy.15.own), channel_id=1, source_target_pairs={{0,1},{1,2},{2,3},{3,4},{4,5},{5,6},{6,7},{7,8},{8,9},{9,10},{10,1... | collective-permute-start | bytes 6291464 | tf_op jit(solution)/shard_map/ppermute | solution.py:167
  26.0 1.3 collective-permute-start.1
  27.3 0.0 copy-done.1
  27.3 0.0 copy-start.3
  27.3 0.0 copy-start.2
  27.3 4.1 %reshape.38 = bf16[256,2,32,64]{3,2,1,0:T(8,128)(2,1)} reshape(bf16[128,2,4096]{2,1,0:T(2,128)(2,1)S(1)} %copy-done.1) | data formatting | bytes 4194304 | tf_op jit(solution)/shard_map/reshape | solution.py:175
  31.4 0.0 copy-done.3
  31.4 0.1 copy.10
  31.5 0.7 reshape.34.cols
  32.2 0.0 copy-done.2
  32.2 1.8 copy.11
  34.1 3.3 reshape.35.slots
  37.4 64.0 %reshape.36 = bf16[2048,64,2,32]{3,2,1,0:T(2,128)(2,1)} reshape(bf16[128,16,4096]{2,1,0:T(8,128)(2,1)} %param.5) | data formatting | bytes 33554432 | tf_op jit(solution)/shard_map/reshape | solution.py:173
  101.4 106.7 %copy.12 = bf16[2048,32,2,64]{0,3,2,1:T(8,128)(2,1)} copy(bf16[2048,32,2,64]{1,2,3,0:T(2,128)(2,1)} %bitcast.2) | data formatting | bytes 33554432 | tf_op jit(solution)/shard_map/transpose | solution.py:172
  208.1 23.6 %copy.17.a_ref = bf16[2048,32,128]{2,1,0:T(8,128)(2,1)} copy(bf16[2048,32,128]{0,2,1:T(8,128)(2,1)} %bitcast.10) | data formatting | bytes 33554432 | tf_op jit(solution)/shard_map/reshape | solution.py:174
  231.8 4.9 %copy.13 = bf16[256,32,2,64]{0,3,2,1:T(8,128)(2,1)S(1)} copy(bf16[256,32,2,64]{3,1,2,0:T(8,128)(2,1)} %bitcast.11) | data formatting | bytes 4194304 | tf_op jit(solution)/shard_map/transpose | solution.py:175
  236.6 3.1 copy.18.p_ref
  239.8 0.0 collective-permute-done.low
  239.8 0.0 collective-permute-done.1.high
  239.8 48.7 %terms.1 = bf16[512,32,128]{2,1,0:T(8,128)(2,1)} custom-call(s32[2048]{0:T(1024)} %reshape.34.cols, s32[8192]{0:T(1024)} %reshape.35.slots, bf16[2048,32,128]{2,1,0:T(8,128)(2,1)} %copy.17.a_ref, bf16[256,32,128]{2,1,0:T(8,128)(2,1)} %copy.18.p_ref, bf16[256,32,128]{2,1,0:T(8,128)(2,1)} %collective-permute-done.low, bf16[256,32,128]{2,1,0:T(8,128)(2,1)} %copy.15.own, ...), custom_call_target="tpu_custom_call" | custom-call | flops 8589934592 | bytes 25165824 | tf_op jit(solution)/shard_map/terms/pallas_call | solution.py:105
  288.5 0.0 copy-start
  288.5 63.9 %all_to_all.5.arrived = bf16[512,32,128]{2,1,0:T(8,128)(2,1)S(1)} all-to-all(bf16[512,32,128]{2,1,0:T(8,128)(2,1)} %terms.1), channel_id=1, replica_groups=mesh['region'=8,'dev'=16] {'region','dev'}, dimensions={0} | all-to-all | bytes 8388608 | tf_op jit(solution)/shard_map/all_to_all | solution.py:178
  352.4 0.0 copy-done
  352.4 2.7 owner_sums.1
  355.0 0.3 reshape.42
  355.4 1.9 copy.20
  357.2 2.9 reshape.43
  (1 shorter events, 0.0 us)
Async XLA Ops:
  15.6 11.7 %copy-start.1 = (bf16[128,2,4096]{2,1,0:T(2,128)(2,1)S(1)}, bf16[128,2,4096]{2,1,0:T(2,128)(2,1)}, u32[]{:S(2)}) copy-start(bf16[128,2,4096]{2,1,0:T(2,128)(2,1)} %param.7) | copy-start | bytes 6291460
  20.3 219.5 %collective-permute-start = (bf16[256,32,128]{2,1,0:T(8,128)(2,1)}, bf16[256,32,128]{2,1,0:T(8,128)(2,1)}, u32[]{:S(2)}, u32[]{:S(2)}) collective-permute-start(bf16[256,32,128]{2,1,0:T(8,128)(2,1)} %copy.15.own), channel_id=1, source_target_pairs={{0,1},{1,2},{2,3},{3,4},{4,5},{5,6},{6,7},{7,8},{8,9},{9,10},{10,1... | collective-permute-start | bytes 6291464 | tf_op jit(solution)/shard_map/ppermute | solution.py:167
  26.0 213.8 %collective-permute-start.1 = (bf16[256,32,128]{2,1,0:T(8,128)(2,1)}, bf16[256,32,128]{2,1,0:T(8,128)(2,1)}, u32[]{:S(2)}, u32[]{:S(2)}) collective-permute-start(bf16[256,32,128]{2,1,0:T(8,128)(2,1)} %copy.15.own), channel_id=1, source_target_pairs={{1,0},{2,1},{3,2},{4,3},{5,4},{6,5},{7,6},{8,7},{9,8},{10,9},{11,1... | collective-permute-start | bytes 6291464 | tf_op jit(solution)/shard_map/ppermute | solution.py:168
  27.3 4.1 %copy-start.3 = (s32[128,16]{0,1:T(8,128)S(1)}, s32[128,16]{0,1:T(8,128)}, u32[]{:S(2)}) copy-start(s32[128,16]{0,1:T(8,128)} %param.6) | copy-start | bytes 24580
  27.3 4.9 %copy-start.2 = (s32[128,2,16,2]{0,3,2,1:T(2,128)S(1)}, s32[128,2,16,2]{0,3,2,1:T(2,128)}, u32[]{:S(2)}) copy-start(s32[128,2,16,2]{0,3,2,1:T(2,128)} %param.8) | copy-start | bytes 98308
  288.5 63.9 %copy-start = (s32[1,512]{1,0:T(1,128)S(1)}, s32[1,512]{1,0:T(1,128)}, u32[]{:S(2)}) copy-start(s32[1,512]{1,0:T(1,128)} %param.9) | copy-start | bytes 6148

commit v2 on v1

v2 whole, which is shorter than its diff:
```python
import functools

import jax
import jax.numpy as jnp
from jax import lax
from jax.experimental import pallas as pl
from jax.experimental.pallas import tpu as pltpu
from jax.sharding import PartitionSpec as P

B = 64
CAP = 4
SLOTS = 64
HALF = B // 2
WIDE = 2 * B
ROWS_STEP = 8
BATCH = 4
PREP = 16
F32 = jnp.float32
BF16 = jnp.bfloat16


def left_lanes(shape):
    return lax.broadcasted_iota(jnp.int32, shape, len(shape) - 1) < B


def swap_lanes(tile):
    return jnp.concatenate([tile[:, B:], tile[:, :B]], axis=1)


def even_odd(first, second):
    left = left_lanes(first.shape)
    even = jnp.where(left, first, swap_lanes(second))
    odd = jnp.where(left, swap_lanes(first), second)
    return even, odd


def turn_pair(first, second, mixed, turned):
    even, odd = even_odd(first, second)
    mixed[pl.ds(0, HALF, stride=2)] = even
    mixed[pl.ds(1, HALF, stride=2)] = odd
    rows = mixed[...]
    turned[...] = jnp.concatenate([rows, rows], axis=0).T
    top = turned[pl.ds(0, B, stride=2)]
    low = turned[pl.ds(1, B, stride=2)]
    return jnp.where(left_lanes(top.shape), top, low)


def p_kernel(p_ref, plain, turned_out, flat, mixed, turned):
    def one(pair, _):
        for u in range(2):
            row = pair * 2 + u
            value = p_ref[row].astype(F32)
            for r in range(HALF):
                flat[u, pl.ds(2 * r, 2)] = value[:, r * WIDE : (r + 1) * WIDE]
            first = flat[u, pl.ds(0, HALF, stride=2)]
            second = flat[u, pl.ds(1, HALF, stride=2)]
            plain[row] = jnp.concatenate([first, second], axis=0).astype(BF16)
            turned_out[row] = turn_pair(first, second, mixed.at[u], turned.at[u]).astype(BF16)
        return 0

    lax.fori_loop(0, PREP // 2, one, 0, unroll=2)


def p_tiles_of(p_vals):
    rows = p_vals.shape[0]
    block = pl.BlockSpec((PREP, B, WIDE), lambda i: (i, 0, 0))
    return pl.pallas_call(
        p_kernel,
        grid=(rows // PREP,),
        in_specs=[pl.BlockSpec((PREP,) + p_vals.shape[1:], lambda i: (i, 0, 0))],
        out_specs=[block, block],
        out_shape=[jax.ShapeDtypeStruct((rows, B, WIDE), BF16)] * 2,
        scratch_shapes=[
            pltpu.VMEM((2, B, WIDE), F32),
            pltpu.VMEM((2, B, WIDE), F32),
            pltpu.VMEM((2, WIDE, WIDE), F32),
        ],
        name="p_tiles",
    )(p_vals)


def a_kernel(a_ref, out, flat):
    a_blocks = a_ref.shape[1]

    def one(pair, _):
        for u in range(2):
            row = pair * 2 + u
            value = a_ref[row].astype(F32)
            for half in range(a_blocks // 8):
                for r in range(HALF):
                    flat[u, pl.ds((half * HALF + r) * 8, 8)] = value[
                        half * 8 : half * 8 + 8, r * WIDE : (r + 1) * WIDE
                    ]
            for k in range(0, a_blocks, 2):
                at = (k // 8) * HALF * 8 + k % 8
                first = flat[u, pl.ds(at, HALF, stride=8)]
                second = flat[u, pl.ds(at + 1, HALF, stride=8)]
                even, odd = even_odd(first, second)
                turned = jnp.concatenate([even, odd, even, odd], axis=0).T.astype(BF16)
                out[row * a_blocks + k] = turned[:B]
                out[row * a_blocks + k + 1] = turned[B:]
        return 0

    lax.fori_loop(0, PREP // 2, one, 0)


def a_tiles_of(a_vals):
    rows, a_blocks, area = a_vals.shape
    return pl.pallas_call(
        a_kernel,
        grid=(rows // PREP,),
        in_specs=[pl.BlockSpec((PREP, a_blocks, area), lambda i: (i, 0, 0))],
        out_specs=pl.BlockSpec((PREP * a_blocks, B, WIDE), lambda i: (i, 0, 0)),
        out_shape=jax.ShapeDtypeStruct((rows * a_blocks, B, WIDE), BF16),
        scratch_shapes=[pltpu.VMEM((2, a_blocks * HALF, WIDE), F32)],
        compiler_params=pltpu.CompilerParams(vmem_limit_bytes=48 * 2**20),
        cost_estimate=pl.CostEstimate(flops=2**33, bytes_accessed=48 * 2**20, transcendentals=0),
        name="a_tiles",
    )(a_vals)


def spread(tile):
    other = swap_lanes(tile)
    left = left_lanes(tile.shape)
    zero = jnp.zeros_like(tile)
    return jnp.concatenate(
        [
            jnp.where(left, tile, zero),
            jnp.where(left, other, zero),
            jnp.where(left, zero, other),
            jnp.where(left, zero, tile),
        ],
        axis=0,
    )


def terms_kernel(a_blocks, cols, slots, a_ref, p_ref, low, own, high, out, right, inner, acc0, acc1, acc2, acc3, sems):
    step = pl.program_id(0)
    rows = own.shape[0]
    accs = ((acc0, acc1), (acc2, acc3))
    copies = [
        pltpu.make_async_copy(source, right.at[pl.ds(n * rows, rows)], sems.at[n])
        for n, source in enumerate((low, own, high))
    ]

    @pl.when(step == 0)
    def _():
        for copy in copies:
            copy.start()

        def clear(n, _):
            for pair in accs:
                for acc in pair:
                    acc[n] = jnp.zeros((HALF, WIDE), F32)
            return 0

        lax.fori_loop(0, out.shape[0], clear, 0, unroll=4)
        for copy in copies:
            copy.wait()

    left = left_lanes((B, WIDE))
    zero = jnp.zeros((B, WIDE), BF16)

    def inner_tiles(row):
        first = (step * ROWS_STEP + row) * a_blocks
        for k in range(a_blocks):
            tile = a_ref[row * a_blocks + k]
            tile = jnp.concatenate(
                [jnp.where(left, tile, zero), jnp.where(left, zero, tile)], axis=0
            )
            lhs = right[cols[first + k]]
            inner[row, pl.ds(k * B, B)] = jnp.dot(
                lhs, tile, preferred_element_type=F32
            ).astype(BF16)

    def add_terms(row):
        first = (step * ROWS_STEP + row) * a_blocks
        weights = jnp.concatenate(
            [spread(p_ref[row, pl.ds(0, HALF)]), spread(p_ref[row, pl.ds(HALF, HALF)])], axis=1
        )
        for start in range(0, a_blocks, BATCH):
            terms = jnp.dot(
                inner[row, pl.ds(start * B, BATCH * B)], weights, preferred_element_type=F32
            )
            for k in range(BATCH):
                at = (first + start + k) * 4
                where = [[slots[at + 2 * q + p] for p in range(2)] for q in range(2)]
                old = [[accs[q][p][where[q][p]] for p in range(2)] for q in range(2)]
                for q in range(2):
                    for p in range(2):
                        top = k * B + p * HALF
                        part = terms[top : top + HALF, q * WIDE : (q + 1) * WIDE]
                        accs[q][p][where[q][p]] = old[q][p] + part

    for row in range(ROWS_STEP):
        inner_tiles(row)
    for row in range(ROWS_STEP):
        add_terms(row)

    @pl.when(step == pl.num_programs(0) - 1)
    def _():
        def finish(n, _):
            out[n] = ((acc0[n] + acc1[n]) + (acc2[n] + acc3[n])).astype(BF16)
            return 0

        lax.fori_loop(0, out.shape[0], finish, 0, unroll=4)


def bucket_sums(a_tiles, cols, slots, p_tiles, low, own, high, buckets):
    row_total = p_tiles.shape[0]
    a_blocks = a_tiles.shape[0] // row_total
    return pl.pallas_call(
        functools.partial(terms_kernel, a_blocks),
        grid_spec=pltpu.PrefetchScalarGridSpec(
            num_scalar_prefetch=2,
            grid=(row_total // ROWS_STEP,),
            in_specs=[
                pl.BlockSpec((ROWS_STEP * a_blocks, B, WIDE), lambda i, *_: (i, 0, 0)),
                pl.BlockSpec((ROWS_STEP, B, WIDE), lambda i, *_: (i, 0, 0)),
                pl.BlockSpec(memory_space=pl.ANY),
                pl.BlockSpec(memory_space=pl.ANY),
                pl.BlockSpec(memory_space=pl.ANY),
            ],
            out_specs=pl.BlockSpec((buckets, HALF, WIDE), lambda i, *_: (0, 0, 0)),
            scratch_shapes=[pltpu.VMEM((3 * row_total, B, WIDE), BF16)]
            + [pltpu.VMEM((ROWS_STEP, a_blocks * B, WIDE), BF16)]
            + [pltpu.VMEM((buckets, HALF, WIDE), F32)] * 4
            + [pltpu.SemaphoreType.DMA((3,))],
        ),
        out_shape=jax.ShapeDtypeStruct((buckets, HALF, WIDE), BF16),
        compiler_params=pltpu.CompilerParams(
            dimension_semantics=("arbitrary",), vmem_limit_bytes=58 * 2**20
        ),
        cost_estimate=pl.CostEstimate(
            flops=2**33, bytes_accessed=24 * 2**20, transcendentals=0
        ),
        name="terms",
    )(cols, slots, a_tiles, p_tiles, low, own, high)


def owner_kernel(places, arrived, out, sums, mixed, turned, flat):
    sums[...] = jnp.zeros_like(sums)

    def add(n, _):
        place = places[n]
        sums[place] += arrived[n].astype(F32)
        return 0

    lax.fori_loop(0, arrived.shape[0], add, 0, unroll=8)

    def turn(group, _):
        for u in range(4):
            slot = group * 8 + 2 * u
            pair = turn_pair(sums[slot], sums[slot + 1], mixed.at[u], turned.at[u])
            for n in range(2):
                flat[pl.ds(2 * u + n, HALF, stride=8)] = pair[n * HALF : (n + 1) * HALF]
        for r in range(HALF):
            out[pl.ds(group * 8, 8), pl.ds(r * WIDE, WIDE)] = flat[pl.ds(r * 8, 8)]
        return 0

    lax.fori_loop(0, SLOTS // 8, turn, 0)


def owner_sums(places, arrived):
    return pl.pallas_call(
        owner_kernel,
        in_specs=[
            pl.BlockSpec(memory_space=pltpu.SMEM),
            pl.BlockSpec(memory_space=pltpu.VMEM),
        ],
        out_specs=pl.BlockSpec(memory_space=pltpu.VMEM),
        out_shape=jax.ShapeDtypeStruct((SLOTS, B * B), F32),
        scratch_shapes=[
            pltpu.VMEM((SLOTS, HALF, WIDE), F32),
            pltpu.VMEM((4, B, WIDE), F32),
            pltpu.VMEM((4, WIDE, WIDE), F32),
            pltpu.VMEM((8 * HALF, WIDE), F32),
        ],
        compiler_params=pltpu.CompilerParams(vmem_limit_bytes=32 * 2**20),
        name="owner_sums",
    )(places, arrived)


def shards(a_vals, a_cols, p_vals, send_slot, recv_slot):
    rows, a_blocks, tile_area = a_vals.shape
    owners = lax.axis_size("region") * lax.axis_size("dev")
    buckets = owners * CAP
    count = lax.axis_size("dev")

    plain, turned = p_tiles_of(p_vals)
    forward = [(i, i + 1) for i in range(count - 1)]
    low = lax.ppermute(turned, "dev", forward)
    high = lax.ppermute(turned, "dev", [(t, s) for s, t in forward])

    cols = (a_cols - (lax.axis_index("dev") - 1) * rows).reshape(-1)
    slots = jnp.transpose(send_slot, (0, 2, 1, 3)).reshape(-1)
    a_tiles = a_tiles_of(a_vals)
    totals = bucket_sums(a_tiles, cols, slots, plain, low, turned, high, buckets)

    arrived = lax.all_to_all(
        totals, ("region", "dev"), split_axis=0, concat_axis=0, tiled=True
    )
    return owner_sums(recv_slot.reshape(-1), arrived)


def solution(mesh):
    in_specs = (
        P(("region", "dev"), None, None),
        P(("region", "dev"), None),
        P(("region", "dev"), None, None),
        P(("region", "dev"), None, None, None),
        P(("region", "dev"), None),
    )
    out_specs = P(("region", "dev"), None)
    return jax.shard_map(shards, mesh=mesh, in_specs=in_specs, out_specs=out_specs, check_vma=False)
```

time: 366 us -> 185 us (0.51); the launches traced: 360 us -> 185 us
  local copies, waits for them, and re-layouts: 238 us -> 5.96 us
  Pallas kernels: 51.4 us -> 105 us
    transpose x4 -> x0, local copies, waits for them, and re-layouts: 121 us -> none  [the longest x1 107 us: shards(): jnp.transpose(a_vals.reshape(rows * a_blocks, B, 2, HALF), (0, 3, 2, 1))]
    reshape x8 -> x0, local copies, waits for them, and re-layouts: 111 us -> none  [the longest x1 64 us: shards(): a_vals.reshape(rows * a_blocks, B, 2, HALF)]
    pallas_call x1 -> x3, Pallas kernels: 2.66 us -> 57 us  [the longest x1 38.2 us: a_tiles_of(): pl.pallas_call(a_kernel, grid=(rows // PREP,), in_specs=[pl.BlockSpec((PR...]
  transfers between devices with their start and end apart: 2 -> 2, of which waited for: 0 -> 0; matrix products, arithmetic and copies ran while one was open for 59% -> 3% of each run, Pallas kernels for 0% -> 21%
where the time goes in v2:
time: 185 us
  Pallas kernels  105 us (57%)
  blocking collectives  66.1 us (36%)
  starting transfers between devices  7.63 us (4%)
  local copies, waits for them, and re-layouts  5.96 us (3%)
    all_to_all x1, blocking collectives, shards(): lax.all_to_all(totals, ('region', 'dev'), split_axis=0, concat_axis=0, ti...  66.1 us
    pallas_call x1, Pallas kernels, bucket_sums(): pl.pallas_call(functools.partial(terms_kernel, a_blocks), grid_spec=pltpu...  48.4 us
    pallas_call x1, Pallas kernels, a_tiles_of(): pl.pallas_call(a_kernel, grid=(rows // PREP,), in_specs=[pl.BlockSpec((PR...  38.2 us
    pallas_call x1, Pallas kernels, p_tiles_of(): pl.pallas_call(p_kernel, grid=(rows // PREP,), in_specs=[pl.BlockSpec((PR...  13.1 us
    ppermute x1, starting transfers between devices, shards(): low = lax.ppermute(turned, 'dev', forward)  6.35 us
    pallas_call x1, Pallas kernels, owner_sums(): pl.pallas_call(owner_kernel, in_specs=[pl.BlockSpec(memory_space=pltpu.SM...  5.71 us
  transfers between devices with their start and end apart: 2, of which 0 were waited for; matrix products, arithmetic and copies ran while one was open for 3% of the time, Pallas kernels for 21%

profile of v2, /device:TPU:1, one launch (start us, length us, event | category | flops | bytes accessed | tf_op | source)
XLA Modules:
  0.0 185.1 jit_solution(2391169241299302386)
XLA Ops:
  0.0 0.0 copy-start.2
  0.0 0.0 copy-start.1
  0.0 13.1 %p_tiles.1 = (bf16[128,64,128]{2,1,0:T(8,128)(2,1)}, bf16[128,64,128]{2,1,0:T(8,128)(2,1)}) custom-call(bf16[128,2,4096]{2,1,0:T(2,128)(2,1)} %p_ref.1), custom_call_target="tpu_custom_call" | custom-call | tf_op jit(solution)/shard_map/p_tiles/pallas_call | solution.py:67
  13.1 1.3 collective-permute-start.1
  14.4 6.3 %collective-permute-start = (bf16[128,64,128]{2,1,0:T(8,128)(2,1)}, bf16[128,64,128]{2,1,0:T(8,128)(2,1)}, u32[]{:S(2)}, u32[]{:S(2)}) collective-permute-start(bf16[128,64,128]{2,1,0:T(8,128)(2,1)} %get-tuple-element.8.own), channel_id=1, source_target_pairs={{0,1},{1,2},{2,3},{3,4},{4,5},{5,6},{6,7},{7,8},{8,9},{9,10},{10,1... | collective-permute-start | bytes 6291464 | tf_op jit(solution)/shard_map/ppermute | solution.py:292
  20.8 0.0 copy-done.2
  20.8 0.1 copy.6
  20.9 0.7 reshape.10.cols
  21.6 0.0 copy-done.1
  21.6 1.8 copy.7
  23.4 3.3 %reshape.11.slots = s32[8192]{0:T(1024)} reshape(s32[128,16,2,2]{3,2,1,0:T(2,128)S(1)} %copy.7) | data formatting | bytes 65536 | tf_op jit(solution)/shard_map/reshape | solution.py:296
  26.8 38.2 %a_tiles.1.a_ref = bf16[2048,64,128]{2,1,0:T(8,128)(2,1)} custom-call(bf16[128,16,4096]{2,1,0:T(8,128)(2,1)} %a_ref.1), custom_call_target="tpu_custom_call" | custom-call | flops 8589934592 | bytes 50331648 | tf_op jit(solution)/shard_map/a_tiles/pallas_call | solution.py:109
  64.9 0.0 collective-permute-done.1.high
  64.9 0.0 collective-permute-done.low
  64.9 48.4 %terms.1 = bf16[512,32,128]{2,1,0:T(8,128)(2,1)} custom-call(s32[2048]{0:T(1024)} %reshape.10.cols, s32[8192]{0:T(1024)} %reshape.11.slots, bf16[2048,64,128]{2,1,0:T(8,128)(2,1)} %a_tiles.1.a_ref, bf16[128,64,128]{2,1,0:T(8,128)(2,1)} %get-tuple-element.7.p_ref, bf16[128,64,128]{2,1,0:T(8,128)(2,1)} %collective-permute-done.low, ...), custom_call_target="tpu_custom_call" | custom-call | flops 8589934592 | bytes 25165824 | tf_op jit(solution)/shard_map/terms/pallas_call | solution.py:212
  113.3 0.0 copy-start
  113.3 66.1 %all_to_all.5.arrived = bf16[512,32,128]{2,1,0:T(8,128)(2,1)S(1)} all-to-all(bf16[512,32,128]{2,1,0:T(8,128)(2,1)} %terms.1), channel_id=1, replica_groups=mesh['region'=8,'dev'=16] {'region','dev'}, dimensions={0} | all-to-all | bytes 8388608 | tf_op jit(solution)/shard_map/all_to_all | solution.py:300
  179.4 0.0 copy-done
  179.4 5.7 %owner_sums.1 = f32[64,4096]{1,0:T(8,128)} custom-call(s32[512]{0:T(512)S(1)} %bitcast.2, bf16[512,32,128]{2,1,0:T(8,128)(2,1)S(1)} %all_to_all.5.arrived), custom_call_target="tpu_custom_call" | custom-call | tf_op jit(solution)/shard_map/owner_sums/pallas_call | solution.py:265
  (1 shorter events, 0.0 us)
Async XLA Ops:
  0.0 20.8 %copy-start.2 = (s32[128,16]{0,1:T(8,128)S(1)}, s32[128,16]{0,1:T(8,128)}, u32[]{:S(2)}) copy-start(s32[128,16]{0,1:T(8,128)} %param.6) | copy-start | bytes 24580
  0.0 21.6 %copy-start.1 = (s32[128,2,16,2]{0,3,2,1:T(2,128)S(1)}, s32[128,2,16,2]{0,3,2,1:T(2,128)}, u32[]{:S(2)}) copy-start(s32[128,2,16,2]{0,3,2,1:T(2,128)} %param.8) | copy-start | bytes 98308
  13.1 51.8 %collective-permute-start.1 = (bf16[128,64,128]{2,1,0:T(8,128)(2,1)}, bf16[128,64,128]{2,1,0:T(8,128)(2,1)}, u32[]{:S(2)}, u32[]{:S(2)}) collective-permute-start(bf16[128,64,128]{2,1,0:T(8,128)(2,1)} %get-tuple-element.8.own), channel_id=1, source_target_pairs={{1,0},{2,1},{3,2},{4,3},{5,4},{6,5},{7,6},{8,7},{9,8},{10,9},{11,1... | collective-permute-start | bytes 6291464 | tf_op jit(solution)/shard_map/ppermute | solution.py:293
  14.4 50.5 %collective-permute-start = (bf16[128,64,128]{2,1,0:T(8,128)(2,1)}, bf16[128,64,128]{2,1,0:T(8,128)(2,1)}, u32[]{:S(2)}, u32[]{:S(2)}) collective-permute-start(bf16[128,64,128]{2,1,0:T(8,128)(2,1)} %get-tuple-element.8.own), channel_id=1, source_target_pairs={{0,1},{1,2},{2,3},{3,4},{4,5},{5,6},{6,7},{7,8},{8,9},{9,10},{10,1... | collective-permute-start | bytes 6291464 | tf_op jit(solution)/shard_map/ppermute | solution.py:292
  113.3 66.1 %copy-start = (s32[1,512]{1,0:T(1,128)S(1)}, s32[1,512]{1,0:T(1,128)}, u32[]{:S(2)}) copy-start(s32[1,512]{1,0:T(1,128)} %param.9) | copy-start | bytes 6148

commit v3 on v2

--- a/solution.py
+++ b/solution.py
@@ -58,7 +58,7 @@
             turned_out[row] = turn_pair(first, second, mixed.at[u], turned.at[u]).astype(BF16)
         return 0
 
-    lax.fori_loop(0, PREP // 2, one, 0, unroll=2)
+    lax.fori_loop(0, PREP // 2, one, 0, unroll=4)
 
 
 def p_tiles_of(p_vals):
@@ -101,7 +101,7 @@
                 out[row * a_blocks + k + 1] = turned[B:]
         return 0
 
-    lax.fori_loop(0, PREP // 2, one, 0)
+    lax.fori_loop(0, PREP // 2, one, 0, unroll=2)
 
 
 def a_tiles_of(a_vals):
@@ -137,6 +137,7 @@
 def terms_kernel(a_blocks, cols, slots, a_ref, p_ref, low, own, high, out, right, inner, acc0, acc1, acc2, acc3, sems):
     step = pl.program_id(0)
     rows = own.shape[0]
+    shift = (lax.axis_index("dev") - 1) * rows
     accs = ((acc0, acc1), (acc2, acc3))
     copies = [
         pltpu.make_async_copy(source, right.at[pl.ds(n * rows, rows)], sems.at[n])
@@ -162,19 +163,19 @@
     zero = jnp.zeros((B, WIDE), BF16)
 
     def inner_tiles(row):
-        first = (step * ROWS_STEP + row) * a_blocks
+        fine = step * ROWS_STEP + row
         for k in range(a_blocks):
             tile = a_ref[row * a_blocks + k]
             tile = jnp.concatenate(
                 [jnp.where(left, tile, zero), jnp.where(left, zero, tile)], axis=0
             )
-            lhs = right[cols[first + k]]
+            lhs = right[cols[k * rows + fine] - shift]
             inner[row, pl.ds(k * B, B)] = jnp.dot(
                 lhs, tile, preferred_element_type=F32
             ).astype(BF16)
 
     def add_terms(row):
-        first = (step * ROWS_STEP + row) * a_blocks
+        fine = step * ROWS_STEP + row
         weights = jnp.concatenate(
             [spread(p_ref[row, pl.ds(0, HALF)]), spread(p_ref[row, pl.ds(HALF, HALF)])], axis=1
         )
@@ -183,8 +184,13 @@
                 inner[row, pl.ds(start * B, BATCH * B)], weights, preferred_element_type=F32
             )
             for k in range(BATCH):
-                at = (first + start + k) * 4
-                where = [[slots[at + 2 * q + p] for p in range(2)] for q in range(2)]
+                where = [
+                    [
+                        slots[((q * a_blocks + start + k) * 2 + p) * rows + fine]
+                        for p in range(2)
+                    ]
+                    for q in range(2)
+                ]
                 old = [[accs[q][p][where[q][p]] for p in range(2)] for q in range(2)]
                 for q in range(2):
                     for p in range(2):
@@ -292,8 +298,8 @@
     low = lax.ppermute(turned, "dev", forward)
     high = lax.ppermute(turned, "dev", [(t, s) for s, t in forward])
 
-    cols = (a_cols - (lax.axis_index("dev") - 1) * rows).reshape(-1)
-    slots = jnp.transpose(send_slot, (0, 2, 1, 3)).reshape(-1)
+    cols = jnp.transpose(a_cols).reshape(-1)
+    slots = jnp.transpose(send_slot, (1, 2, 3, 0)).reshape(-1)
     a_tiles = a_tiles_of(a_vals)
     totals = bucket_sums(a_tiles, cols, slots, plain, low, turned, high, buckets)
 

time: 185 us -> 184 us (level)
  waiting for transfers between devices: 0.01 us -> 11 us
  Pallas kernels: 105 us -> 97.4 us
  local copies, waits for them, and re-layouts: 5.96 us -> 1.34 us
    ppermute x1, waiting for transfers between devices: 0.01 us -> 10.1 us  [shards(): high = lax.ppermute(turned, 'dev', [(t, s) for s, t in forward])]
    pallas_call x1, Pallas kernels: 38.2 us -> 33.4 us  [a_tiles_of(): pl.pallas_call(a_kernel, grid=(rows // PREP,), in_specs=[pl.BlockSpec((PR...]
    reshape x2 -> x0, local copies, waits for them, and re-layouts: 4.01 us -> none  [the longest x1 3.33 us: shards(): slots = jnp.transpose(send_slot, (0, 2, 1, 3)).reshape(-1)]
    pallas_call x1, Pallas kernels: 13.1 us -> 9.84 us  [p_tiles_of(): pl.pallas_call(p_kernel, grid=(rows // PREP,), in_specs=[pl.BlockSpec((PR...]
  transfers between devices with their start and end apart: 2 -> 2, of which waited for: 0 -> 2; matrix products, arithmetic and copies ran while one was open for 3% -> 0% of each run, Pallas kernels for 21% -> 18%
where the time goes in v3:
time: 184 us; the launch traced here: 183 us
  Pallas kernels  97.4 us (53%)
  blocking collectives  66.9 us (36%)
  waiting for transfers between devices  11 us (6%)
  starting transfers between devices  6.41 us (3%)
    all_to_all x1, blocking collectives, shards(): lax.all_to_all(totals, ('region', 'dev'), split_axis=0, concat_axis=0, ti...  66.9 us
    pallas_call x1, Pallas kernels, bucket_sums(): pl.pallas_call(functools.partial(terms_kernel, a_blocks), grid_spec=pltpu...  48.4 us
    pallas_call x1, Pallas kernels, a_tiles_of(): pl.pallas_call(a_kernel, grid=(rows // PREP,), in_specs=[pl.BlockSpec((PR...  33.4 us
    ppermute x1, waiting for transfers between devices, shards(): high = lax.ppermute(turned, 'dev', [(t, s) for s, t in forward])  10.1 us
    pallas_call x1, Pallas kernels, p_tiles_of(): pl.pallas_call(p_kernel, grid=(rows // PREP,), in_specs=[pl.BlockSpec((PR...  9.84 us
    pallas_call x1, Pallas kernels, owner_sums(): pl.pallas_call(owner_kernel, in_specs=[pl.BlockSpec(memory_space=pltpu.SM...  5.71 us
    ppermute x1, starting transfers between devices, shards(): low = lax.ppermute(turned, 'dev', forward)  5.13 us
  transfers between devices with their start and end apart: 2, of which 2 were waited for; matrix products, arithmetic and copies ran while one was open for 0% of the time, Pallas kernels for 18%

profile of v3, /device:TPU:1, one launch (start us, length us, event | category | flops | bytes accessed | tf_op | source)
XLA Modules:
  0.0 183.1 jit_solution(13967579938634533887)
XLA Ops:
  0.0 9.8 %p_tiles.1 = (bf16[128,64,128]{2,1,0:T(8,128)(2,1)}, bf16[128,64,128]{2,1,0:T(8,128)(2,1)}) custom-call(bf16[128,2,4096]{2,1,0:T(2,128)(2,1)} %p_ref.1), custom_call_target="tpu_custom_call" | custom-call | tf_op jit(solution)/shard_map/p_tiles/pallas_call | solution.py:67
  9.8 1.3 collective-permute-start.1
  11.1 5.1 %collective-permute-start = (bf16[128,64,128]{2,1,0:T(8,128)(2,1)}, bf16[128,64,128]{2,1,0:T(8,128)(2,1)S(1)}, u32[]{:S(2)}, u32[]{:S(2)}) collective-permute-start(bf16[128,64,128]{2,1,0:T(8,128)(2,1)} %get-tuple-element.8.own), channel_id=1, source_target_pairs={{0,1},{1,2},{2,3},{3,4},{4,5},{5,6},{6,7},{7,8},{8,9},{9,10},{10,1... | collective-permute-start | bytes 6291464 | tf_op jit(solution)/shard_map/ppermute | solution.py:298
  16.3 33.4 %a_tiles.1.a_ref = bf16[2048,64,128]{2,1,0:T(8,128)(2,1)} custom-call(bf16[128,16,4096]{2,1,0:T(8,128)(2,1)} %a_ref.1), custom_call_target="tpu_custom_call" | custom-call | flops 8589934592 | bytes 50331648 | tf_op jit(solution)/shard_map/a_tiles/pallas_call | solution.py:109
  49.7 10.1 %collective-permute-done.1.high = bf16[128,64,128]{2,1,0:T(8,128)(2,1)S(1)} collective-permute-done((bf16[128,64,128]{2,1,0:T(8,128)(2,1)}, bf16[128,64,128]{2,1,0:T(8,128)(2,1)S(1)}, u32[]{:S(2)}, u32[]{:S(2)}) %collective-permute-start.1) | collective-permute-done | bytes 2097184 | tf_op jit(solution)/shard_map/ppermute | solution.py:299
  59.7 0.0 copy-start.1
  59.7 1.0 collective-permute-done.low
  60.7 0.0 copy-start.2
  60.7 0.3 copy-done.1
  61.0 1.0 copy-done.2
  62.0 48.4 %terms.1 = bf16[512,32,128]{2,1,0:T(8,128)(2,1)} custom-call(s32[2048]{0:T(1024)} %bitcast.9, s32[8192]{0:T(1024)} %bitcast.8, bf16[2048,64,128]{2,1,0:T(8,128)(2,1)} %a_tiles.1.a_ref, bf16[128,64,128]{2,1,0:T(8,128)(2,1)} %get-tuple-element.7.p_ref, bf16[128,64,128]{2,1,0:T(8,128)(2,1)} %copy-done.2, bf16[128,64,128]{2,1,0:T(8,128)(2,1)} %get-tuple-element.8.own, ...), custom_call_target="tpu_custom_call" | custom-call | flops 8589934592 | bytes 25165824 | tf_op jit(solution)/shard_map/terms/pallas_call | solution.py:218
  110.5 0.0 copy-start
  110.5 66.9 %all_to_all.5.arrived = bf16[512,32,128]{2,1,0:T(8,128)(2,1)S(1)} all-to-all(bf16[512,32,128]{2,1,0:T(8,128)(2,1)} %terms.1), channel_id=1, replica_groups=mesh['region'=8,'dev'=16] {'region','dev'}, dimensions={0} | all-to-all | bytes 8388608 | tf_op jit(solution)/shard_map/all_to_all | solution.py:306
  177.4 0.0 copy-done
  177.4 5.7 %owner_sums.1 = f32[64,4096]{1,0:T(8,128)} custom-call(s32[512]{0:T(512)S(1)} %bitcast.7, bf16[512,32,128]{2,1,0:T(8,128)(2,1)S(1)} %all_to_all.5.arrived), custom_call_target="tpu_custom_call" | custom-call | tf_op jit(solution)/shard_map/owner_sums/pallas_call | solution.py:271
Async XLA Ops:
  9.8 49.9 %collective-permute-start.1 = (bf16[128,64,128]{2,1,0:T(8,128)(2,1)}, bf16[128,64,128]{2,1,0:T(8,128)(2,1)S(1)}, u32[]{:S(2)}, u32[]{:S(2)}) collective-permute-start(bf16[128,64,128]{2,1,0:T(8,128)(2,1)} %get-tuple-element.8.own), channel_id=1, source_target_pairs={{1,0},{2,1},{3,2},{4,3},{5,4},{6,5},{7,6},{8,7},{9,8},{10,9},{11,1... | collective-permute-start | bytes 6291464 | tf_op jit(solution)/shard_map/ppermute | solution.py:299
  11.1 49.6 %collective-permute-start = (bf16[128,64,128]{2,1,0:T(8,128)(2,1)}, bf16[128,64,128]{2,1,0:T(8,128)(2,1)S(1)}, u32[]{:S(2)}, u32[]{:S(2)}) collective-permute-start(bf16[128,64,128]{2,1,0:T(8,128)(2,1)} %get-tuple-element.8.own), channel_id=1, source_target_pairs={{0,1},{1,2},{2,3},{3,4},{4,5},{5,6},{6,7},{7,8},{8,9},{9,10},{10,1... | collective-permute-start | bytes 6291464 | tf_op jit(solution)/shard_map/ppermute | solution.py:298
  59.7 1.3 copy-start.1
  60.7 1.3 copy-start.2
  110.5 66.9 %copy-start = (s32[1,512]{1,0:T(1,128)S(1)}, s32[1,512]{1,0:T(1,128)}, u32[]{:S(2)}) copy-start(s32[1,512]{1,0:T(1,128)} %param.9) | copy-start | bytes 6148

commit v4 on v3

--- a/solution.py
+++ b/solution.py
@@ -45,78 +45,119 @@
     return jnp.where(left_lanes(top.shape), top, low)
 
 
-def p_kernel(p_ref, plain, turned_out, flat, mixed, turned):
-    def one(pair, _):
-        for u in range(2):
-            row = pair * 2 + u
-            value = p_ref[row].astype(F32)
+def p_rows(p_ref, plain, turned_out, flat, mixed, turned, pair):
+    for u in range(2):
+        row = pair * 2 + u
+        value = p_ref[row].astype(F32)
+        for r in range(HALF):
+            flat[u, pl.ds(2 * r, 2)] = value[:, r * WIDE : (r + 1) * WIDE]
+        first = flat[u, pl.ds(0, HALF, stride=2)]
+        second = flat[u, pl.ds(1, HALF, stride=2)]
+        plain[row] = jnp.concatenate([first, second], axis=0).astype(BF16)
+        turned_out[row] = turn_pair(first, second, mixed.at[u], turned.at[u]).astype(BF16)
+
+
+def a_rows(a_ref, out, flat, pair):
+    a_blocks = a_ref.shape[1]
+    for u in range(2):
+        row = pair * 2 + u
+        value = a_ref[row].astype(F32)
+        for half in range(a_blocks // 8):
             for r in range(HALF):
-                flat[u, pl.ds(2 * r, 2)] = value[:, r * WIDE : (r + 1) * WIDE]
-            first = flat[u, pl.ds(0, HALF, stride=2)]
-            second = flat[u, pl.ds(1, HALF, stride=2)]
-            plain[row] = jnp.concatenate([first, second], axis=0).astype(BF16)
-            turned_out[row] = turn_pair(first, second, mixed.at[u], turned.at[u]).astype(BF16)
+                flat[u, pl.ds((half * HALF + r) * 8, 8)] = value[
+                    half * 8 : half * 8 + 8, r * WIDE : (r + 1) * WIDE
+                ]
+        for k in range(0, a_blocks, 2):
+            at = (k // 8) * HALF * 8 + k % 8
+            even, odd = even_odd(
+                flat[u, pl.ds(at, HALF, stride=8)], flat[u, pl.ds(at + 1, HALF, stride=8)]
+            )
+            turned = jnp.concatenate([even, odd, even, odd], axis=0).T.astype(BF16)
+            out[row * a_blocks + k] = turned[:B]
+            out[row * a_blocks + k + 1] = turned[B:]
+
+
+def tiles_kernel(
+    p_ref, a_hbm, plain, own, low, high, a_out, flat_p, mixed, turned, flat_a, sent, got
+):
+    rows, a_blocks, area = a_hbm.shape
+    count = lax.axis_size("dev")
+    region, me = lax.axis_index("region"), lax.axis_index("dev")
+    after, before = lax.rem(me + 1, count), lax.rem(me + count - 1, count)
+    sides = ((after, low), (before, high))
+
+    barrier = pltpu.get_barrier_semaphore()
+    for other in (after, before):
+        pl.semaphore_signal(
+            barrier, inc=1, device_id=(region, other), device_id_type=pl.DeviceIdType.MESH
+        )
+    pl.semaphore_wait(barrier, 2)
+
+    def halo(side, first, size):
+        other, target = sides[side]
+        return pltpu.make_async_remote_copy(
+            src_ref=own.at[pl.ds(first, size)],
+            dst_ref=target.at[pl.ds(first, size)],
+            send_sem=sent.at[side],
+            recv_sem=got.at[side],
+            device_id=(region, other),
+            device_id_type=pl.DeviceIdType.MESH,
+        )
+
+    def p_step(chunk, _):
+        def one(n, _):
+            p_rows(p_ref, plain, own, flat_p, mixed, turned, chunk * (PREP // 2) + n)
+            return 0
+
+        lax.fori_loop(0, PREP // 2, one, 0, unroll=4)
+        for side in range(2):
+            halo(side, chunk * PREP, PREP).start()
         return 0
 
-    lax.fori_loop(0, PREP // 2, one, 0, unroll=4)
-
-
-def p_tiles_of(p_vals):
-    rows = p_vals.shape[0]
-    block = pl.BlockSpec((PREP, B, WIDE), lambda i: (i, 0, 0))
+    lax.fori_loop(0, rows // PREP, p_step, 0)
+
+    def a_step(a_ref, out):
+        def one(n, _):
+            a_rows(a_ref, out, flat_a, n)
+            return 0
+
+        lax.fori_loop(0, PREP // 2, one, 0, unroll=2)
+
+    pltpu.emit_pipeline(
+        a_step,
+        grid=(rows // PREP,),
+        in_specs=[pl.BlockSpec((PREP, a_blocks, area), lambda i: (i, 0, 0))],
+        out_specs=[pl.BlockSpec((PREP * a_blocks, B, WIDE), lambda i: (i, 0, 0))],
+    )(a_hbm, a_out)
+
+    for side in range(2):
+        halo(side, 0, rows).wait()
+
+
+def tiles_of(p_vals, a_vals):
+    rows, a_blocks, _ = a_vals.shape
+    vmem = pl.BlockSpec(memory_space=pltpu.VMEM)
+    anywhere = pl.BlockSpec(memory_space=pl.ANY)
+    tiles = jax.ShapeDtypeStruct((rows, B, WIDE), BF16)
     return pl.pallas_call(
-        p_kernel,
-        grid=(rows // PREP,),
-        in_specs=[pl.BlockSpec((PREP,) + p_vals.shape[1:], lambda i: (i, 0, 0))],
-        out_specs=[block, block],
-        out_shape=[jax.ShapeDtypeStruct((rows, B, WIDE), BF16)] * 2,
+        tiles_kernel,
+        in_specs=[vmem, anywhere],
+        out_specs=[vmem, vmem, anywhere, anywhere, anywhere],
+        out_shape=[tiles] * 4 + [jax.ShapeDtypeStruct((rows * a_blocks, B, WIDE), BF16)],
         scratch_shapes=[
             pltpu.VMEM((2, B, WIDE), F32),
             pltpu.VMEM((2, B, WIDE), F32),
             pltpu.VMEM((2, WIDE, WIDE), F32),
+            pltpu.VMEM((2, a_blocks * HALF, WIDE), F32),
+            pltpu.SemaphoreType.DMA((2,)),
+            pltpu.SemaphoreType.DMA((2,)),
         ],
-        name="p_tiles",
-    )(p_vals)
-
-
-def a_kernel(a_ref, out, flat):
-    a_blocks = a_ref.shape[1]
-
-    def one(pair, _):
-        for u in range(2):
-            row = pair * 2 + u
-            value = a_ref[row].astype(F32)
-            for half in range(a_blocks // 8):
-                for r in range(HALF):
-                    flat[u, pl.ds((half * HALF + r) * 8, 8)] = value[
-                        half * 8 : half * 8 + 8, r * WIDE : (r + 1) * WIDE
-                    ]
-            for k in range(0, a_blocks, 2):
-                at = (k // 8) * HALF * 8 + k % 8
-                first = flat[u, pl.ds(at, HALF, stride=8)]
-                second = flat[u, pl.ds(at + 1, HALF, stride=8)]
-                even, odd = even_odd(first, second)
-                turned = jnp.concatenate([even, odd, even, odd], axis=0).T.astype(BF16)
-                out[row * a_blocks + k] = turned[:B]
-                out[row * a_blocks + k + 1] = turned[B:]
-        return 0
-
-    lax.fori_loop(0, PREP // 2, one, 0, unroll=2)
-
-
-def a_tiles_of(a_vals):
-    rows, a_blocks, area = a_vals.shape
-    return pl.pallas_call(
-        a_kernel,
-        grid=(rows // PREP,),
-        in_specs=[pl.BlockSpec((PREP, a_blocks, area), lambda i: (i, 0, 0))],
-        out_specs=pl.BlockSpec((PREP * a_blocks, B, WIDE), lambda i: (i, 0, 0)),
-        out_shape=jax.ShapeDtypeStruct((rows * a_blocks, B, WIDE), BF16),
-        scratch_shapes=[pltpu.VMEM((2, a_blocks * HALF, WIDE), F32)],
-        compiler_params=pltpu.CompilerParams(vmem_limit_bytes=48 * 2**20),
-        cost_estimate=pl.CostEstimate(flops=2**33, bytes_accessed=48 * 2**20, transcendentals=0),
-        name="a_tiles",
-    )(a_vals)
+        compiler_params=pltpu.CompilerParams(
+            collective_id=0, has_side_effects=True, vmem_limit_bytes=48 * 2**20
+        ),
+        cost_estimate=pl.CostEstimate(flops=2**33, bytes_accessed=56 * 2**20, transcendentals=0),
+        name="tiles",
+    )(p_vals, a_vals)
 
 
 def spread(tile):
@@ -291,17 +332,11 @@
     rows, a_blocks, tile_area = a_vals.shape
     owners = lax.axis_size("region") * lax.axis_size("dev")
     buckets = owners * CAP
-    count = lax.axis_size("dev")
-
-    plain, turned = p_tiles_of(p_vals)
-    forward = [(i, i + 1) for i in range(count - 1)]
-    low = lax.ppermute(turned, "dev", forward)
-    high = lax.ppermute(turned, "dev", [(t, s) for s, t in forward])
-
+
+    plain, own, low, high, a_tiles = tiles_of(p_vals, a_vals)
     cols = jnp.transpose(a_cols).reshape(-1)
     slots = jnp.transpose(send_slot, (1, 2, 3, 0)).reshape(-1)
-    a_tiles = a_tiles_of(a_vals)
-    totals = bucket_sums(a_tiles, cols, slots, plain, low, turned, high, buckets)
+    totals = bucket_sums(a_tiles, cols, slots, plain, low, own, high, buckets)
 
     arrived = lax.all_to_all(
         totals, ("region", "dev"), split_axis=0, concat_axis=0, tiled=True

time: 184 us -> 174 us (0.946)
  Pallas kernels: 97.4 us -> 109 us
  waiting for transfers between devices: 11 us -> 0 us
  starting transfers between devices: 6.41 us -> 0 us
  blocking collectives: 66.9 us -> 62.5 us
    pallas_call x2 -> x1, Pallas kernels: 43.3 us -> 54.6 us  [tiles_of(): pl.pallas_call(tiles_kernel, in_specs=[vmem, anywhere], out_specs=[vmem,...]
    ppermute x2 -> x0, waiting for transfers between devices: 11 us -> none  [the longest x1 10.1 us: shards(): high = lax.ppermute(turned, 'dev', [(t, s) for s, t in forward])]
    ppermute x2 -> x0, starting transfers between devices: 6.41 us -> none  [the longest x1 5.13 us: shards(): low = lax.ppermute(turned, 'dev', forward)]
    all_to_all x1, blocking collectives: 66.9 us -> 62.5 us  [shards(): lax.all_to_all(totals, ('region', 'dev'), split_axis=0, concat_axis=0, ti...]
  transfers between devices with their start and end apart: 2 -> 0, of which waited for: 2 -> 0; matrix products, arithmetic and copies ran while one was open for 0% -> 0% of each run, Pallas kernels for 18% -> 0%
where the time goes in v4:
time: 174 us
  Pallas kernels  109 us (63%)
  blocking collectives  62.5 us (36%)
  local copies, waits for them, and re-layouts  2.64 us (2%)
    all_to_all x1, blocking collectives, shards(): lax.all_to_all(totals, ('region', 'dev'), split_axis=0, concat_axis=0, ti...  62.5 us
    pallas_call x1, Pallas kernels, tiles_of(): pl.pallas_call(tiles_kernel, in_specs=[vmem, anywhere], out_specs=[vmem,...  54.6 us
    pallas_call x1, Pallas kernels, bucket_sums(): pl.pallas_call(functools.partial(terms_kernel, a_blocks), grid_spec=pltpu...  48.4 us
    pallas_call x1, Pallas kernels, owner_sums(): pl.pallas_call(owner_kernel, in_specs=[pl.BlockSpec(memory_space=pltpu.SM...  5.71 us

profile of v4, /device:TPU:1, one launch (start us, length us, event | category | flops | bytes accessed | tf_op | source)
XLA Modules:
  0.0 173.9 jit_solution(3754659290975350829)
XLA Ops:
  0.0 54.6 %tiles.1 = (bf16[128,64,128]{2,1,0:T(8,128)(2,1)S(1)}, bf16[128,64,128]{2,1,0:T(8,128)(2,1)S(1)}, bf16[128,64,128]{2,1,0:T(8,128)(2,1)}, bf16[128,64,128]{2,1,0:T(8,128)(2,1)}, bf16[2048,64,128]{2,1,0:T(8,128)(2,1)}) custom-call(bf16[128,2,4096]{2,1,0:T(2,128)(2,1)} %p_ref.1, bf16[128,16,4096]{2,1,0:T(8,128)(2,1)} %a_hbm.1), custom_call_target="tpu_custom_call" | custom-call | flops 8589934592 | bytes 58720256 | tf_op jit(solution)/shard_map/tiles/pallas_call | solution.py:142
  54.6 0.0 copy-start
  54.6 1.3 copy-done
  56.0 0.0 copy-start.1
  56.0 1.3 copy-done.1
  57.2 48.4 %terms.1 = bf16[512,32,128]{2,1,0:T(8,128)(2,1)} custom-call(s32[2048]{0:T(1024)} %bitcast.9, s32[8192]{0:T(1024)} %bitcast.8, bf16[2048,64,128]{2,1,0:T(8,128)(2,1)} %get-tuple-element.10.a_ref, bf16[128,64,128]{2,1,0:T(8,128)(2,1)} %copy-done, bf16[128,64,128]{2,1,0:T(8,128)(2,1)} %get-tuple-element.12.low, bf16[128,64,128]{2,1,0:T(8,128)(2,1)} %copy-done.1, ...), custom_call_target="tpu_custom_call" | custom-call | flops 8589934592 | bytes 25165824 | tf_op jit(solution)/shard_map/terms/pallas_call | solution.py:259
  105.7 0.0 copy-start.2
  105.7 62.5 %all_to_all.5.arrived = bf16[512,32,128]{2,1,0:T(8,128)(2,1)S(1)} all-to-all(bf16[512,32,128]{2,1,0:T(8,128)(2,1)} %terms.1), channel_id=1, replica_groups=mesh['region'=8,'dev'=16] {'region','dev'}, dimensions={0} | all-to-all | bytes 8388608 | tf_op jit(solution)/shard_map/all_to_all | solution.py:341
  168.2 0.0 copy-done.2
  168.2 5.7 %owner_sums.1 = f32[64,4096]{1,0:T(8,128)} custom-call(s32[512]{0:T(512)S(1)} %bitcast.7, bf16[512,32,128]{2,1,0:T(8,128)(2,1)S(1)} %all_to_all.5.arrived), custom_call_target="tpu_custom_call" | custom-call | tf_op jit(solution)/shard_map/owner_sums/pallas_call | solution.py:312
Async XLA Ops:
  54.6 1.3 copy-start
  56.0 1.3 copy-start.1
  105.7 62.5 %copy-start.2 = (s32[1,512]{1,0:T(1,128)S(1)}, s32[1,512]{1,0:T(1,128)}, u32[]{:S(2)}) copy-start(s32[1,512]{1,0:T(1,128)} %param.9) | copy-start | bytes 6148

commit v5 on v4

--- a/solution.py
+++ b/solution.py
@@ -15,6 +15,7 @@
 ROWS_STEP = 8
 BATCH = 4
 PREP = 16
+PIECES = 4
 F32 = jnp.float32
 BF16 = jnp.bfloat16
 
@@ -78,7 +79,8 @@
 
 
 def tiles_kernel(
-    p_ref, a_hbm, plain, own, low, high, a_out, flat_p, mixed, turned, flat_a, sent, got
+    p_ref, a_hbm, plain_out, own_out, low, high, a_out, plain, own, flat_p, mixed, turned,
+    flat_a, sent, got, kept
 ):
     rows, a_blocks, area = a_hbm.shape
     count = lax.axis_size("dev")
@@ -104,6 +106,12 @@
             device_id_type=pl.DeviceIdType.MESH,
         )
 
+    def keep(which, first, size):
+        source, target = ((plain, plain_out), (own, own_out))[which]
+        return pltpu.make_async_copy(
+            source.at[pl.ds(first, size)], target.at[pl.ds(first, size)], kept.at[which]
+        )
+
     def p_step(chunk, _):
         def one(n, _):
             p_rows(p_ref, plain, own, flat_p, mixed, turned, chunk * (PREP // 2) + n)
@@ -112,6 +120,7 @@
         lax.fori_loop(0, PREP // 2, one, 0, unroll=4)
         for side in range(2):
             halo(side, chunk * PREP, PREP).start()
+            keep(side, chunk * PREP, PREP).start()
         return 0
 
     lax.fori_loop(0, rows // PREP, p_step, 0)
@@ -131,6 +140,7 @@
     )(a_hbm, a_out)
 
     for side in range(2):
+        keep(side, 0, rows).wait()
         halo(side, 0, rows).wait()
 
 
@@ -142,18 +152,21 @@
     return pl.pallas_call(
         tiles_kernel,
         in_specs=[vmem, anywhere],
-        out_specs=[vmem, vmem, anywhere, anywhere, anywhere],
+        out_specs=[pl.BlockSpec(memory_space=pltpu.HBM)] * 5,
         out_shape=[tiles] * 4 + [jax.ShapeDtypeStruct((rows * a_blocks, B, WIDE), BF16)],
         scratch_shapes=[
+            pltpu.VMEM((rows, B, WIDE), BF16),
+            pltpu.VMEM((rows, B, WIDE), BF16),
             pltpu.VMEM((2, B, WIDE), F32),
             pltpu.VMEM((2, B, WIDE), F32),
             pltpu.VMEM((2, WIDE, WIDE), F32),
             pltpu.VMEM((2, a_blocks * HALF, WIDE), F32),
             pltpu.SemaphoreType.DMA((2,)),
             pltpu.SemaphoreType.DMA((2,)),
+            pltpu.SemaphoreType.DMA((2,)),
         ],
         compiler_params=pltpu.CompilerParams(
-            collective_id=0, has_side_effects=True, vmem_limit_bytes=48 * 2**20
+            collective_id=0, has_side_effects=True, vmem_limit_bytes=62 * 2**20
         ),
         cost_estimate=pl.CostEstimate(flops=2**33, bytes_accessed=56 * 2**20, transcendentals=0),
         name="tiles",
@@ -175,7 +188,7 @@
     )
 
 
-def terms_kernel(a_blocks, cols, slots, a_ref, p_ref, low, own, high, out, right, inner, acc0, acc1, acc2, acc3, sems):
+def terms_kernel(a_blocks, cols, slots, a_ref, p_ref, low, own, high, out, right, inner, done, acc0, acc1, acc2, acc3, sems):
     step = pl.program_id(0)
     rows = own.shape[0]
     shift = (lax.axis_index("dev") - 1) * rows
@@ -196,7 +209,7 @@
                     acc[n] = jnp.zeros((HALF, WIDE), F32)
             return 0
 
-        lax.fori_loop(0, out.shape[0], clear, 0, unroll=4)
+        lax.fori_loop(0, done.shape[0], clear, 0, unroll=4)
         for copy in copies:
             copy.wait()
 
@@ -246,11 +259,22 @@
 
     @pl.when(step == pl.num_programs(0) - 1)
     def _():
-        def finish(n, _):
-            out[n] = ((acc0[n] + acc1[n]) + (acc2[n] + acc3[n])).astype(BF16)
-            return 0
-
-        lax.fori_loop(0, out.shape[0], finish, 0, unroll=4)
+        leaving = []
+        for piece in range(PIECES):
+            size = done.shape[0] // PIECES
+
+            def finish(n, _):
+                n = piece * size + n
+                done[n] = ((acc0[n] + acc1[n]) + (acc2[n] + acc3[n])).astype(BF16)
+                return 0
+
+            lax.fori_loop(0, size, finish, 0, unroll=4)
+            part = pl.ds(piece * size, size)
+            copy = pltpu.make_async_copy(done.at[part], out.at[part], sems.at[3 + piece])
+            copy.start()
+            leaving.append(copy)
+        for copy in leaving:
+            copy.wait()
 
 
 def bucket_sums(a_tiles, cols, slots, p_tiles, low, own, high, buckets):
@@ -268,11 +292,12 @@
                 pl.BlockSpec(memory_space=pl.ANY),
                 pl.BlockSpec(memory_space=pl.ANY),
             ],
-            out_specs=pl.BlockSpec((buckets, HALF, WIDE), lambda i, *_: (0, 0, 0)),
+            out_specs=pl.BlockSpec(memory_space=pl.ANY),
             scratch_shapes=[pltpu.VMEM((3 * row_total, B, WIDE), BF16)]
             + [pltpu.VMEM((ROWS_STEP, a_blocks * B, WIDE), BF16)]
+            + [pltpu.VMEM((buckets, HALF, WIDE), BF16)]
             + [pltpu.VMEM((buckets, HALF, WIDE), F32)] * 4
-            + [pltpu.SemaphoreType.DMA((3,))],
+            + [pltpu.SemaphoreType.DMA((3 + PIECES,))],
         ),
         out_shape=jax.ShapeDtypeStruct((buckets, HALF, WIDE), BF16),
         compiler_params=pltpu.CompilerParams(
@@ -285,20 +310,27 @@
     )(cols, slots, a_tiles, p_tiles, low, own, high)
 
 
-def owner_kernel(places, arrived, out, sums, mixed, turned, flat):
-    sums[...] = jnp.zeros_like(sums)
+def owner_kernel(places, arrived, out, sum0, sum1, sum2, sum3, mixed, turned, flat):
+    sums = (sum0, sum1, sum2, sum3)
+    for part in sums:
+        part[...] = jnp.zeros_like(part)
 
     def add(n, _):
-        place = places[n]
-        sums[place] += arrived[n].astype(F32)
+        at = [places[4 * n + u] for u in range(4)]
+        old = [sums[u][at[u]] for u in range(4)]
+        for u in range(4):
+            sums[u][at[u]] = old[u] + arrived[4 * n + u].astype(F32)
         return 0
 
-    lax.fori_loop(0, arrived.shape[0], add, 0, unroll=8)
+    lax.fori_loop(0, arrived.shape[0] // 4, add, 0, unroll=4)
+
+    def total(slot):
+        return (sum0[slot] + sum1[slot]) + (sum2[slot] + sum3[slot])
 
     def turn(group, _):
         for u in range(4):
             slot = group * 8 + 2 * u
-            pair = turn_pair(sums[slot], sums[slot + 1], mixed.at[u], turned.at[u])
+            pair = turn_pair(total(slot), total(slot + 1), mixed.at[u], turned.at[u])
             for n in range(2):
                 flat[pl.ds(2 * u + n, HALF, stride=8)] = pair[n * HALF : (n + 1) * HALF]
         for r in range(HALF):
@@ -318,7 +350,7 @@
         out_specs=pl.BlockSpec(memory_space=pltpu.VMEM),
         out_shape=jax.ShapeDtypeStruct((SLOTS, B * B), F32),
         scratch_shapes=[
-            pltpu.VMEM((SLOTS, HALF, WIDE), F32),
+            *[pltpu.VMEM((SLOTS, HALF, WIDE), F32)] * 4,
             pltpu.VMEM((4, B, WIDE), F32),
             pltpu.VMEM((4, WIDE, WIDE), F32),
             pltpu.VMEM((8 * HALF, WIDE), F32),

time: 174 us -> 170 us (0.977)
  local copies, waits for them, and re-layouts: 2.64 us -> 0.01 us
  Pallas kernels: 109 us -> 107 us
    unnamed x6 -> x2, local copies, waits for them, and re-layouts: 2.64 us -> 0.01 us
where the time goes in v5:
time: 170 us
  Pallas kernels  107 us (63%)
  blocking collectives  62.4 us (37%)
    all_to_all x1, blocking collectives, shards(): lax.all_to_all(totals, ('region', 'dev'), split_axis=0, concat_axis=0, ti...  62.4 us
    pallas_call x1, Pallas kernels, tiles_of(): pl.pallas_call(tiles_kernel, in_specs=[vmem, anywhere], out_specs=[pl.Blo...  54.6 us
    pallas_call x1, Pallas kernels, bucket_sums(): pl.pallas_call(functools.partial(terms_kernel, a_blocks), grid_spec=pltpu...  47.5 us
    pallas_call x1, Pallas kernels, owner_sums(): pl.pallas_call(owner_kernel, in_specs=[pl.BlockSpec(memory_space=pltpu.SM...  5.03 us

profile of v5, /device:TPU:1, one launch (start us, length us, event | category | flops | bytes accessed | tf_op | source)
XLA Modules:
  0.0 169.6 jit_solution(12057887433879519724)
XLA Ops:
  0.0 54.6 %tiles.1 = (bf16[128,64,128]{2,1,0:T(8,128)(2,1)}, bf16[128,64,128]{2,1,0:T(8,128)(2,1)}, bf16[128,64,128]{2,1,0:T(8,128)(2,1)}, bf16[128,64,128]{2,1,0:T(8,128)(2,1)}, bf16[2048,64,128]{2,1,0:T(8,128)(2,1)}) custom-call(bf16[128,2,4096]{2,1,0:T(2,128)(2,1)} %p_ref.1, bf16[128,16,4096]{2,1,0:T(8,128)(2,1)} %a_hbm.1), custom_call_target="tpu_custom_call" | custom-call | flops 8589934592 | bytes 58720256 | tf_op jit(solution)/shard_map/tiles/pallas_call | solution.py:152
  54.6 47.5 %terms.1 = bf16[512,32,128]{2,1,0:T(8,128)(2,1)} custom-call(s32[2048]{0:T(1024)} %bitcast.9, s32[8192]{0:T(1024)} %bitcast.8, bf16[2048,64,128]{2,1,0:T(8,128)(2,1)} %get-tuple-element.10.a_ref, bf16[128,64,128]{2,1,0:T(8,128)(2,1)} %get-tuple-element.11.p_ref, bf16[128,64,128]{2,1,0:T(8,128)(2,1)} %get-tuple-element.12.low, ...), custom_call_target="tpu_custom_call" | custom-call | flops 8589934592 | bytes 25165824 | tf_op jit(solution)/shard_map/terms/pallas_call | solution.py:283
  102.1 0.0 copy-start
  102.1 62.4 %all_to_all.5.arrived = bf16[512,32,128]{2,1,0:T(8,128)(2,1)S(1)} all-to-all(bf16[512,32,128]{2,1,0:T(8,128)(2,1)} %terms.1), channel_id=1, replica_groups=mesh['region'=8,'dev'=16] {'region','dev'}, dimensions={0} | all-to-all | bytes 8388608 | tf_op jit(solution)/shard_map/all_to_all | solution.py:373
  164.6 0.0 copy-done
  164.6 5.0 %owner_sums.1 = f32[64,4096]{1,0:T(8,128)} custom-call(s32[512]{0:T(512)S(1)} %bitcast.7, bf16[512,32,128]{2,1,0:T(8,128)(2,1)S(1)} %all_to_all.5.arrived), custom_call_target="tpu_custom_call" | custom-call | tf_op jit(solution)/shard_map/owner_sums/pallas_call | solution.py:344
Async XLA Ops:
  102.1 62.5 %copy-start = (s32[1,512]{1,0:T(1,128)S(1)}, s32[1,512]{1,0:T(1,128)}, u32[]{:S(2)}) copy-start(s32[1,512]{1,0:T(1,128)} %param.9) | copy-start | bytes 6148

commit v6 on v5

--- a/solution.py
+++ b/solution.py
@@ -15,6 +15,7 @@
 ROWS_STEP = 8
 BATCH = 4
 PREP = 16
+A_STEP = 8
 PIECES = 4
 F32 = jnp.float32
 BF16 = jnp.bfloat16
@@ -130,13 +131,13 @@
             a_rows(a_ref, out, flat_a, n)
             return 0
 
-        lax.fori_loop(0, PREP // 2, one, 0, unroll=2)
+        lax.fori_loop(0, A_STEP // 2, one, 0, unroll=2)
 
     pltpu.emit_pipeline(
         a_step,
-        grid=(rows // PREP,),
-        in_specs=[pl.BlockSpec((PREP, a_blocks, area), lambda i: (i, 0, 0))],
-        out_specs=[pl.BlockSpec((PREP * a_blocks, B, WIDE), lambda i: (i, 0, 0))],
+        grid=(rows // A_STEP,),
+        in_specs=[pl.BlockSpec((A_STEP, a_blocks, area), lambda i: (i, 0, 0))],
+        out_specs=[pl.BlockSpec((A_STEP * a_blocks, B, WIDE), lambda i: (i, 0, 0))],
     )(a_hbm, a_out)
 
     for side in range(2):
@@ -209,7 +210,7 @@
                     acc[n] = jnp.zeros((HALF, WIDE), F32)
             return 0
 
-        lax.fori_loop(0, done.shape[0], clear, 0, unroll=4)
+        lax.fori_loop(0, done.shape[0], clear, 0, unroll=8)
         for copy in copies:
             copy.wait()
 
@@ -268,7 +269,7 @@
                 done[n] = ((acc0[n] + acc1[n]) + (acc2[n] + acc3[n])).astype(BF16)
                 return 0
 
-            lax.fori_loop(0, size, finish, 0, unroll=4)
+            lax.fori_loop(0, size, finish, 0, unroll=8)
             part = pl.ds(piece * size, size)
             copy = pltpu.make_async_copy(done.at[part], out.at[part], sems.at[3 + piece])
             copy.start()

time: 170 us -> 170 us (level)
  no operation moved by 1% of the time
where the time goes in v6:
time: 170 us; the launch traced here: 169 us
  Pallas kernels  107 us (63%)
  blocking collectives  62.5 us (37%)
    all_to_all x1, blocking collectives, shards(): lax.all_to_all(totals, ('region', 'dev'), split_axis=0, concat_axis=0, ti...  62.5 us
    pallas_call x1, Pallas kernels, tiles_of(): pl.pallas_call(tiles_kernel, in_specs=[vmem, anywhere], out_specs=[pl.Blo...  54.6 us
    pallas_call x1, Pallas kernels, bucket_sums(): pl.pallas_call(functools.partial(terms_kernel, a_blocks), grid_spec=pltpu...  47.1 us
    pallas_call x1, Pallas kernels, owner_sums(): pl.pallas_call(owner_kernel, in_specs=[pl.BlockSpec(memory_space=pltpu.SM...  5.03 us

profile of v6, /device:TPU:1, one launch (start us, length us, event | category | flops | bytes accessed | tf_op | source)
XLA Modules:
  0.0 169.3 jit_solution(6206761230356936761)
XLA Ops:
  0.0 54.6 %tiles.1 = (bf16[128,64,128]{2,1,0:T(8,128)(2,1)}, bf16[128,64,128]{2,1,0:T(8,128)(2,1)}, bf16[128,64,128]{2,1,0:T(8,128)(2,1)}, bf16[128,64,128]{2,1,0:T(8,128)(2,1)}, bf16[2048,64,128]{2,1,0:T(8,128)(2,1)}) custom-call(bf16[128,2,4096]{2,1,0:T(2,128)(2,1)} %p_ref.1, bf16[128,16,4096]{2,1,0:T(8,128)(2,1)} %a_hbm.1), custom_call_target="tpu_custom_call" | custom-call | flops 8589934592 | bytes 58720256 | tf_op jit(solution)/shard_map/tiles/pallas_call | solution.py:153
  54.6 47.1 %terms.1 = bf16[512,32,128]{2,1,0:T(8,128)(2,1)} custom-call(s32[2048]{0:T(1024)} %bitcast.9, s32[8192]{0:T(1024)} %bitcast.8, bf16[2048,64,128]{2,1,0:T(8,128)(2,1)} %get-tuple-element.10.a_ref, bf16[128,64,128]{2,1,0:T(8,128)(2,1)} %get-tuple-element.11.p_ref, bf16[128,64,128]{2,1,0:T(8,128)(2,1)} %get-tuple-element.12.low, ...), custom_call_target="tpu_custom_call" | custom-call | flops 8589934592 | bytes 25165824 | tf_op jit(solution)/shard_map/terms/pallas_call | solution.py:284
  101.8 0.0 copy-start
  101.8 62.5 %all_to_all.5.arrived = bf16[512,32,128]{2,1,0:T(8,128)(2,1)S(1)} all-to-all(bf16[512,32,128]{2,1,0:T(8,128)(2,1)} %terms.1), channel_id=1, replica_groups=mesh['region'=8,'dev'=16] {'region','dev'}, dimensions={0} | all-to-all | bytes 8388608 | tf_op jit(solution)/shard_map/all_to_all | solution.py:374
  164.3 0.0 copy-done
  164.3 5.0 %owner_sums.1 = f32[64,4096]{1,0:T(8,128)} custom-call(s32[512]{0:T(512)S(1)} %bitcast.7, bf16[512,32,128]{2,1,0:T(8,128)(2,1)S(1)} %all_to_all.5.arrived), custom_call_target="tpu_custom_call" | custom-call | tf_op jit(solution)/shard_map/owner_sums/pallas_call | solution.py:345
Async XLA Ops:
  101.8 62.5 %copy-start = (s32[1,512]{1,0:T(1,128)S(1)}, s32[1,512]{1,0:T(1,128)}, u32[]{:S(2)}) copy-start(s32[1,512]{1,0:T(1,128)} %param.9) | copy-start | bytes 6148
